TPU v7x, 32 devices: a whole 2x2x4 slice. The times are simulated.
32 devices in a mesh: chan: 4 (over z), tm: 8 (over y, x, core).
Axes of the slice: x: 2, y: 2, z: 4, core: 2. Of those that a mesh axis runs over, the one named last changes fastest.
Arguments:
- strain_rate: float32 [1024, 4096], P('chan', 'tm'), may hold values from -64 to 64
Outputs:
- stacks: float32 [32, 2, 13056], P('chan', None, 'tm')
All inputs are finite; a program needn't handle non-finite values.
Results may differ from a plain program's by a relative error of at most 0.0041.
Values may be sent and summed in bfloat16 or wider, within the bound.
No kernel may reach another device: no remote copies, remote signals or barrier semaphores. Data moves between devices by JAX's collectives and lax.ppermute only.
A program may use at most 64 MiB of HBM per device.

v0:
```python
import functools
import math

import jax
import jax.numpy as jnp
from jax import lax
from jax.experimental import pallas as pl
from jax.experimental.pallas import tpu as pltpu
from jax.sharding import PartitionSpec as P

SRC = 8
MAXLAG = 25
W2 = 64
LAGS = 51
FINE = 4
COARSE = -(-LAGS // FINE)
LANES = 128
PAD = 128
CORES = 2


def band_matrix(rows, columns, related):
    p = lax.broadcasted_iota(jnp.int32, (rows, columns), 0)
    t = lax.broadcasted_iota(jnp.int32, (rows, columns), 1)
    return jnp.where(related(p, t), 1.0, 0.0).astype(jnp.bfloat16)


def halves(values):
    high = values.astype(jnp.bfloat16).astype(jnp.float32)
    return high, values - high


def banded_sums(pieces, band):
    height = pieces[0].shape[0]
    parts = [halves(piece) for piece in pieces]
    stacked = jnp.concatenate([p[0] for p in parts] + [p[1] for p in parts], axis=0)
    sums = jnp.dot(
        stacked.astype(jnp.bfloat16), band, preferred_element_type=jnp.float32
    )
    count = len(pieces)
    return [
        sums[c * height : (c + 1) * height]
        + sums[(count + c) * height : (count + c + 1) * height]
        for c in range(count)
    ]


def level(window_sums):
    return window_sums / (2 * W2 + 1) + 1e-05


def rows_for_here(ref, group, chips):
    me = lax.axis_index("tm")
    every = ref.shape[0] // SRC
    pieces = []
    for m in range(chips):
        start = pl.multiple_of((me ^ (CORES * m + 1)) * group, group)
        pieces.append(ref[pl.ds(start, group)])
    pieces += [ref[q * every : q * every + 1] for q in range(SRC)]
    return jnp.concatenate(pieces, axis=0)


def pack_kernel(group, chips, x_ref, out_ref):
    out_ref[...] = rows_for_here(x_ref, group, chips)


def coded_rows(own, other):
    first_core = lax.rem(lax.axis_index("tm"), CORES) == 0
    x = jnp.concatenate(
        [jnp.where(first_core, own, other), jnp.where(first_core, other, own)], axis=1
    )
    height, length = x.shape
    border = jnp.zeros((height, LANES), jnp.float32)
    magnitude = jnp.concatenate([border, jnp.abs(x), border], axis=1)
    inner = min(256, length)
    band = band_matrix(
        inner + 2 * LANES, inner, lambda p, t: jnp.abs(p - LANES - t) <= W2
    )
    sums = jnp.concatenate(
        banded_sums(
            [
                magnitude[:, start : start + inner + 2 * LANES]
                for start in range(0, length, inner)
            ],
            band,
        ),
        axis=1,
    )
    levels = level(sums)
    normed = x / levels
    left = lax.broadcasted_iota(jnp.int32, (height, LANES), 1) < W2
    tail = length - LANES
    ends = jnp.where(left, normed[:, :LANES], normed[:, tail:])
    end_levels = jnp.where(left, levels[:, :LANES], levels[:, tail:])
    coded = jnp.concatenate([normed, halves(ends)[1], end_levels], axis=1)
    return coded.astype(jnp.bfloat16)


def code_sources_kernel(group, chips, own_ref, other_ref, out_ref):
    first = chips * group
    other = rows_for_here(other_ref, group, chips)
    out_ref[...] = coded_rows(own_ref[first:], other[first:])


def code_receivers_kernel(group, chips, own_ref, other_ref, out_ref):
    last = chips * group
    other = rows_for_here(other_ref, group, chips)
    out_ref[...] = coded_rows(own_ref[:last], other[:last])


def join_kernel(offsets, receivers_ref, *refs):
    given, blocks = refs[:offsets], refs[offsets:]
    group = receivers_ref.shape[0] // len(blocks)
    sources = [ref[...].astype(jnp.float32) for ref in given]
    receivers = receivers_ref[...].astype(jnp.float32)
    for m, block in enumerate(blocks):
        rows = [receivers[m * group : (m + 1) * group]] + sources
        block[...] = jnp.concatenate(rows, axis=0).astype(jnp.bfloat16)


def finished_shards(runs, held):
    chips, height, width = held.shape
    length = width - 2 * LANES
    chip = lax.div(lax.axis_index("tm"), CORES)
    for m in range(chips):
        held[chip ^ m] = runs[m]
    left = lax.broadcasted_iota(jnp.int32, (height, LANES), 1) < W2
    tail = length - LANES
    end_values, end_levels = [], []

    def lanes(c, first):
        return held[c, :, first : first + LANES].astype(jnp.float32)

    for c in range(chips):
        high = jnp.where(left, lanes(c, 0), lanes(c, tail))
        end_values.append(high + lanes(c, length))
        end_levels.append(lanes(c, length + LANES))

    def meeting(ends, outside):
        outside = [jnp.full((height, LANES), outside, jnp.float32)]
        return [
            jnp.where(left, after, before)
            for before, after in zip(outside + ends, ends + outside)
        ]

    def across(p, t):
        at_p, at_t = jnp.where(p < W2, p, p - LANES), jnp.where(t < W2, t, t - LANES)
        return ((p < W2) != (t < W2)) & (jnp.abs(at_p - at_t) <= W2)

    values, levels = meeting(end_values, 0.0), meeting(end_levels, 1.0)
    added = banded_sums(
        [jnp.abs(v) * l for v, l in zip(values, levels)],
        band_matrix(LANES, LANES, across),
    )
    ends = [
        v * l / (l + a / (2 * W2 + 1)) for v, l, a in zip(values, levels, added)
    ]
    shard = length // CORES
    padding = jnp.zeros((height, PAD), held.dtype)
    for k in range(chips * CORES):
        c, part = k // CORES, k % CORES
        pieces = [held[c, :, part * shard : (part + 1) * shard], padding]
        if part == 0:
            head = jnp.where(left, ends[c], lanes(c, 0)).astype(held.dtype)
            pieces = [head, held[c, :, LANES:shard], padding]
        if part == CORES - 1:
            last = jnp.where(left, lanes(c, tail), ends[c + 1]).astype(held.dtype)
            pieces = [held[c, :, part * shard : tail], last, padding]
        yield jnp.concatenate(pieces, axis=1)


def correlate_kernel(offsets, scale, *refs):
    chips = len(refs) - offsets - 3
    blocks, refs = refs[:chips], refs[chips:]
    outs, (held, mixed, table) = refs[:offsets], refs[offsets:]
    sources = offsets * SRC
    group = held.shape[1] - sources
    runs = [ref[...].astype(held.dtype) for ref in blocks[:1] + blocks[:0:-1]]
    product = None
    for wide in finished_shards(runs, held):
        receivers, senders = wide[:group], wide[group:]
        fine = [pltpu.roll(receivers, MAXLAG - j, 1) for j in range(FINE)]
        coarse = [
            pltpu.roll(senders, FINE * i, 1) if i else senders for i in range(COARSE)
        ]
        term = lax.dot_general(
            jnp.concatenate(fine, axis=0).astype(jnp.bfloat16),
            jnp.concatenate(coarse, axis=0).astype(jnp.bfloat16),
            (((1,), (1,)), ((), ())),
            preferred_element_type=jnp.float32,
        )
        product = term if product is None else product + term
    product = product * scale
    for h in range(mixed.shape[0]):
        first, last = h * LANES, min((h + 1) * LANES, COARSE * sources)
        for j in range(FINE):
            mixed[h, pl.ds(j, group, stride=FINE), : last - first] = product[
                j * group : (j + 1) * group, first:last
            ]
        table[h * LANES : (h + 1) * LANES] = mixed[h].T.astype(table.dtype)
    lane = lax.broadcasted_iota(jnp.int32, (sources, LANES), 1)
    width = group * LAGS
    tiles = [None] * -(-width // LANES)

    def place(tile, piece, low, high):
        if tiles[tile] is None:
            tiles[tile] = piece
        elif low == 0:
            tiles[tile] = jnp.where(lane < high, piece, tiles[tile])
        else:
            tiles[tile] = jnp.where(lane >= low, piece, tiles[tile])

    for b in range(group):
        column = b * FINE
        for i in range(COARSE):
            piece = table[
                i * sources : (i + 1) * sources,
                column // LANES * LANES : (column // LANES + 1) * LANES,
            ]
            start = b * LAGS + i * FINE
            shift = (start - column) % LANES
            if shift:
                piece = pltpu.roll(piece, shift, 1)
            count = min(FINE, LAGS - i * FINE)
            tile, low = start // LANES, start % LANES
            place(tile, piece, low, LANES)
            if low + count > LANES:
                tiles[tile + 1] = piece
    for tile, value in enumerate(tiles):
        first = tile * LANES
        last = min(first + LANES, width)
        for o in range(offsets):
            rows = value.astype(jnp.float32)[o * SRC : (o + 1) * SRC, : last - first]
            outs[o][:, first:last] = rows.astype(jnp.bfloat16)


def stack_kernel(*refs):
    out_ref = refs[-1]
    for o, ref in enumerate(refs[:-1]):
        out_ref[:, o, :] = ref[...].astype(jnp.float32)


def call(kernel, out_shape, inputs, scratch=(), flops=0):
    single = not isinstance(out_shape, list)
    spec = pl.BlockSpec(memory_space=pltpu.VMEM)
    moved = sum(v.size * v.dtype.itemsize for v in inputs)
    return pl.pallas_call(
        kernel,
        out_shape=out_shape,
        in_specs=[spec] * len(inputs),
        out_specs=spec if single else [spec] * len(out_shape),
        scratch_shapes=list(scratch),
        compiler_params=pltpu.CompilerParams(vmem_limit_bytes=32 * 1024 * 1024),
        cost_estimate=pl.CostEstimate(
            flops=flops, bytes_accessed=moved, transcendentals=0
        ),
    )(*inputs)


def swapped(block, axis, m):
    devices = range(lax.axis_size(axis))
    return lax.ppermute(block, axis, [(k, k ^ m) for k in devices])


def passed_along(block, distance):
    devices = range(lax.axis_size("chan"))
    route = [((i - distance) % len(devices), i) for i in devices]
    return lax.ppermute(block, "chan", route)


def passed_across(block, distance):
    count, places = lax.axis_size("chan"), lax.axis_size("tm")
    route = [
        ((i - distance) % count * places + (k ^ 1), i * places + k)
        for i in range(count)
        for k in range(places)
    ]
    return lax.ppermute(block, ("chan", "tm"), route)


def body(strain_rate):
    channels, length = strain_rate.shape
    shards = lax.axis_size("tm")
    chips = shards // CORES
    reach = lax.axis_size("chan") // 4
    group = channels // shards
    steps = list(range(-reach, 0)) + list(range(1, reach + 1))
    offsets = len(steps)
    sources = offsets * SRC
    scale = 1.0 / math.sqrt(length * shards)
    run = CORES * length
    coded = run + 2 * LANES

    other = swapped(strain_rate, "tm", 1)
    own = call(
        functools.partial(pack_kernel, group, chips),
        jax.ShapeDtypeStruct((chips * group + SRC, length), jnp.float32),
        [strain_rate],
        flops=8 * channels * length,
    )
    own_sources = call(
        functools.partial(code_sources_kernel, group, chips),
        jax.ShapeDtypeStruct((SRC, coded), jnp.bfloat16),
        [own, other],
    )
    arrived = [passed_along(own_sources, d) for d in steps]
    own_receivers = call(
        functools.partial(code_receivers_kernel, group, chips),
        jax.ShapeDtypeStruct((chips * group, coded), jnp.bfloat16),
        [own, other],
        flops=8 * chips * group * run * (256 + 2 * LANES),
    )
    blocks = call(
        functools.partial(join_kernel, offsets),
        [jax.ShapeDtypeStruct((group + sources, coded), jnp.bfloat16)] * chips,
        [own_receivers] + arrived,
    )
    blocks = list(blocks[:1]) + [
        swapped(blocks[m], "tm", CORES * m) for m in range(chips - 1, 0, -1)
    ]
    columns = -(-group * FINE // LANES) * LANES
    heights = -(-COARSE * sources // LANES) * LANES
    kind = jnp.float32 if group % 16 or sources % 16 else jnp.bfloat16
    results = call(
        functools.partial(correlate_kernel, offsets, scale),
        [jax.ShapeDtypeStruct((SRC, group * LAGS), jnp.bfloat16)] * offsets,
        blocks,
        scratch=[
            pltpu.VMEM((chips, group + sources, coded), kind),
            pltpu.VMEM((heights // LANES, columns, LANES), jnp.float32),
            pltpu.VMEM((heights, columns), kind),
        ],
        flops=2 * shards * (length + PAD) * group * FINE * COARSE * sources,
    )
    arrived = [passed_across(r, -d) for r, d in zip(results, steps)]
    return call(
        stack_kernel,
        jax.ShapeDtypeStruct((SRC, offsets, group * LAGS), jnp.float32),
        arrived,
    )


def solution(mesh):
    placed = (P("chan", "tm"),)
    return jax.shard_map(
        body, mesh=mesh, in_specs=placed, out_specs=P("chan", None, "tm"), check_vma=False
    )
```

profile of v0, /device:TPU:0, one launch (start us, length us, event | category | flops | bytes accessed | tf_op | source)
XLA Modules:
  0.0 25.3 jit_solution(15276687362349569247)
XLA Ops:
  0.0 0.5 %collective-permute-start = (f32[256,512]{1,0:T(8,128)}, f32[256,512]{1,0:T(8,128)S(1)}, u32[]{:S(2)}, u32[]{:S(2)}) collective-permute-start(f32[256,512]{1,0:T(8,128)} %x_ref.1), channel_id=1, source_target_pairs={{0,1},{1,0},{2,3},{3,2},{4,5},{5,4},{6,7},{7,6},{8,9},{9,8},{10,11... | collective-permute-start | bytes 1572872 | tf_op jit(solution)/shard_map/ppermute | solution.py:262
  0.5 0.0 copy-start
  0.5 1.0 %copy-done = f32[256,512]{1,0:T(8,128)S(1)} copy-done((f32[256,512]{1,0:T(8,128)S(1)}, f32[256,512]{1,0:T(8,128)}, u32[]{:S(2)}) %copy-start) | copy-done | bytes 524312
  1.5 0.7 %collective-permute-done.other_ref = f32[256,512]{1,0:T(8,128)S(1)} collective-permute-done((f32[256,512]{1,0:T(8,128)}, f32[256,512]{1,0:T(8,128)S(1)}, u32[]{:S(2)}, u32[]{:S(2)}) %collective-permute-start) | collective-permute-done | bytes 524320 | tf_op jit(solution)/shard_map/ppermute | solution.py:262
  2.2 0.2 shard_map.19
  2.4 3.0 %collective-permute-start.2 = (bf16[8,1280]{1,0:T(8,128)(2,1)S(1)}, bf16[8,1280]{1,0:T(8,128)(2,1)S(1)}, u32[]{:S(2)}, u32[]{:S(2)}) collective-permute-start(bf16[8,1280]{1,0:T(8,128)(2,1)S(1)} %shard_map.19), channel_id=1, source_target_pairs={{24,0},{0,8},{8,16},{16,24},{25,1},{1,9},{9,17},{17,25},{26,2},{2,... | collective-permute-start | bytes 61448 | tf_op jit(solution)/shard_map/ppermute | solution.py:268
  5.4 2.1 %collective-permute-start.1 = (bf16[8,1280]{1,0:T(8,128)(2,1)S(1)}, bf16[8,1280]{1,0:T(8,128)(2,1)S(1)}, u32[]{:S(2)}, u32[]{:S(2)}) collective-permute-start(bf16[8,1280]{1,0:T(8,128)(2,1)S(1)} %shard_map.19), channel_id=1, source_target_pairs={{8,0},{16,8},{24,16},{0,24},{9,1},{17,9},{25,17},{1,25},{10,2},{18... | collective-permute-start | bytes 61448 | tf_op jit(solution)/shard_map/ppermute | solution.py:268
  7.5 0.5 %shard_map.18.receivers_ref = bf16[128,1280]{1,0:T(8,128)(2,1)S(1)} custom-call(f32[136,512]{1,0:T(8,128)S(1)} %shard_map.17.own_ref, f32[256,512]{1,0:T(8,128)S(1)} %collective-permute-done.other_ref), custom_call_target="tpu_custom_call" | custom-call | flops 536870912 | bytes 802816 | tf_op jit(solution)/shard_map/pallas_call | solution.py:247
  8.0 1.3 %collective-permute-done.2.refs_1_ = bf16[8,1280]{1,0:T(8,128)(2,1)S(1)} collective-permute-done((bf16[8,1280]{1,0:T(8,128)(2,1)S(1)}, bf16[8,1280]{1,0:T(8,128)(2,1)S(1)}, u32[]{:S(2)}, u32[]{:S(2)}) %collective-permute-start.2) | collective-permute-done | bytes 20512 | tf_op jit(solution)/shard_map/ppermute | solution.py:268
  9.3 0.1 collective-permute-done.1.refs_0_
  9.5 2.5 %collective-permute-start.3 = (bf16[48,1280]{1,0:T(8,128)(2,1)S(1)}, bf16[48,1280]{1,0:T(8,128)(2,1)S(1)}, u32[]{:S(2)}, u32[]{:S(2)}) collective-permute-start(bf16[48,1280]{1,0:T(8,128)(2,1)S(1)} %get-tuple-element.12), channel_id=1, source_target_pairs={{0,6},{1,7},{2,4},{3,5},{4,2},{5,3},{6,0},{7,1},{8,14},{9,15},{10,... | collective-permute-start | bytes 368648 | tf_op jit(solution)/shard_map/ppermute | solution.py:262
  12.0 0.5 %collective-permute-start.4 = (bf16[48,1280]{1,0:T(8,128)(2,1)S(1)}, bf16[48,1280]{1,0:T(8,128)(2,1)S(1)}, u32[]{:S(2)}, u32[]{:S(2)}) collective-permute-start(bf16[48,1280]{1,0:T(8,128)(2,1)S(1)} %get-tuple-element.13), channel_id=1, source_target_pairs={{0,4},{1,5},{2,6},{3,7},{4,0},{5,1},{6,2},{7,3},{8,12},{9,13},{10,... | collective-permute-start | bytes 368648 | tf_op jit(solution)/shard_map/ppermute | solution.py:262
  12.5 0.5 %collective-permute-start.5 = (bf16[48,1280]{1,0:T(8,128)(2,1)S(1)}, bf16[48,1280]{1,0:T(8,128)(2,1)S(1)}, u32[]{:S(2)}, u32[]{:S(2)}) collective-permute-start(bf16[48,1280]{1,0:T(8,128)(2,1)S(1)} %get-tuple-element.14), channel_id=1, source_target_pairs={{0,2},{1,3},{2,0},{3,1},{4,6},{5,7},{6,4},{7,5},{8,10},{9,11},{10,... | collective-permute-start | bytes 368648 | tf_op jit(solution)/shard_map/ppermute | solution.py:262
  13.0 3.1 %collective-permute-done.3.refs_1_ = bf16[48,1280]{1,0:T(8,128)(2,1)S(1)} collective-permute-done((bf16[48,1280]{1,0:T(8,128)(2,1)S(1)}, bf16[48,1280]{1,0:T(8,128)(2,1)S(1)}, u32[]{:S(2)}, u32[]{:S(2)}) %collective-permute-start.3) | collective-permute-done | bytes 122912 | tf_op jit(solution)/shard_map/ppermute | solution.py:262
  16.1 1.2 %collective-permute-done.4.refs_2_ = bf16[48,1280]{1,0:T(8,128)(2,1)S(1)} collective-permute-done((bf16[48,1280]{1,0:T(8,128)(2,1)S(1)}, bf16[48,1280]{1,0:T(8,128)(2,1)S(1)}, u32[]{:S(2)}, u32[]{:S(2)}) %collective-permute-start.4) | collective-permute-done | bytes 122912 | tf_op jit(solution)/shard_map/ppermute | solution.py:262
  17.3 0.2 collective-permute-done.5.refs_3_
  17.5 2.0 %shard_map.21 = (bf16[8,1632]{1,0:T(8,128)(2,1)S(1)}, bf16[8,1632]{1,0:T(8,128)(2,1)S(1)}) custom-call(bf16[48,1280]{1,0:T(8,128)(2,1)S(1)} %get-tuple-element.11.refs_0_, bf16[48,1280]{1,0:T(8,128)(2,1)S(1)} %collective-permute-done.3.refs_1_, bf16[48,1280]{1,0:T(8,128)(2,1)S(1)} %collective-permute-done.4.refs_2_, ...), custom_call_target="tpu_custom_call" | custom-call | flops 272629760 | bytes 491520 | tf_op jit(solution)/shard_map/pallas_call | solution.py:247
  19.5 0.1 collective-permute-start.6
  19.6 3.5 %collective-permute-start.7 = (bf16[8,1632]{1,0:T(8,128)(2,1)S(1)}, bf16[8,1632]{1,0:T(8,128)(2,1)S(1)}, u32[]{:S(2)}, u32[]{:S(2)}) collective-permute-start(bf16[8,1632]{1,0:T(8,128)(2,1)S(1)} %get-tuple-element.16), channel_id=1, source_target_pairs={{9,0},{8,1},{11,2},{10,3},{13,4},{12,5},{15,6},{14,7},{17,8},{16,9... | collective-permute-start | bytes 78344 | tf_op jit(solution)/shard_map/ppermute | solution.py:278
  23.1 1.5 %collective-permute-done.6.refs_0_ = bf16[8,1632]{1,0:T(8,128)(2,1)S(1)} collective-permute-done((bf16[8,1632]{1,0:T(8,128)(2,1)S(1)}, bf16[8,1632]{1,0:T(8,128)(2,1)S(1)}, u32[]{:S(2)}, u32[]{:S(2)}) %collective-permute-start.6) | collective-permute-done | bytes 26144 | tf_op jit(solution)/shard_map/ppermute | solution.py:278
  24.6 0.0 collective-permute-done.7.refs_1_
  24.6 0.7 %shard_map.22 = f32[8,2,1632]{2,1,0:T(2,128)} custom-call(bf16[8,1632]{1,0:T(8,128)(2,1)S(1)} %collective-permute-done.6.refs_0_, bf16[8,1632]{1,0:T(8,128)(2,1)S(1)} %collective-permute-done.7.refs_1_), custom_call_target="tpu_custom_call" | custom-call | bytes 52224 | tf_op jit(solution)/shard_map/pallas_call | solution.py:247
  (2 shorter events, 0.1 us)
Async XLA Ops:
  0.0 2.2 %collective-permute-start = (f32[256,512]{1,0:T(8,128)}, f32[256,512]{1,0:T(8,128)S(1)}, u32[]{:S(2)}, u32[]{:S(2)}) collective-permute-start(f32[256,512]{1,0:T(8,128)} %x_ref.1), channel_id=1, source_target_pairs={{0,1},{1,0},{2,3},{3,2},{4,5},{5,4},{6,7},{7,6},{8,9},{9,8},{10,11... | collective-permute-start | bytes 1572872 | tf_op jit(solution)/shard_map/ppermute | solution.py:262
  0.5 1.0 %copy-start = (f32[256,512]{1,0:T(8,128)S(1)}, f32[256,512]{1,0:T(8,128)}, u32[]{:S(2)}) copy-start(f32[256,512]{1,0:T(8,128)} %x_ref.1) | copy-start | bytes 1572868
  2.4 6.9 %collective-permute-start.2 = (bf16[8,1280]{1,0:T(8,128)(2,1)S(1)}, bf16[8,1280]{1,0:T(8,128)(2,1)S(1)}, u32[]{:S(2)}, u32[]{:S(2)}) collective-permute-start(bf16[8,1280]{1,0:T(8,128)(2,1)S(1)} %shard_map.19), channel_id=1, source_target_pairs={{24,0},{0,8},{8,16},{16,24},{25,1},{1,9},{9,17},{17,25},{26,2},{2,... | collective-permute-start | bytes 61448 | tf_op jit(solution)/shard_map/ppermute | solution.py:268
  5.4 4.0 %collective-permute-start.1 = (bf16[8,1280]{1,0:T(8,128)(2,1)S(1)}, bf16[8,1280]{1,0:T(8,128)(2,1)S(1)}, u32[]{:S(2)}, u32[]{:S(2)}) collective-permute-start(bf16[8,1280]{1,0:T(8,128)(2,1)S(1)} %shard_map.19), channel_id=1, source_target_pairs={{8,0},{16,8},{24,16},{0,24},{9,1},{17,9},{25,17},{1,25},{10,2},{18... | collective-permute-start | bytes 61448 | tf_op jit(solution)/shard_map/ppermute | solution.py:268
  9.5 6.7 %collective-permute-start.3 = (bf16[48,1280]{1,0:T(8,128)(2,1)S(1)}, bf16[48,1280]{1,0:T(8,128)(2,1)S(1)}, u32[]{:S(2)}, u32[]{:S(2)}) collective-permute-start(bf16[48,1280]{1,0:T(8,128)(2,1)S(1)} %get-tuple-element.12), channel_id=1, source_target_pairs={{0,6},{1,7},{2,4},{3,5},{4,2},{5,3},{6,0},{7,1},{8,14},{9,15},{10,... | collective-permute-start | bytes 368648 | tf_op jit(solution)/shard_map/ppermute | solution.py:262
  12.0 5.4 %collective-permute-start.4 = (bf16[48,1280]{1,0:T(8,128)(2,1)S(1)}, bf16[48,1280]{1,0:T(8,128)(2,1)S(1)}, u32[]{:S(2)}, u32[]{:S(2)}) collective-permute-start(bf16[48,1280]{1,0:T(8,128)(2,1)S(1)} %get-tuple-element.13), channel_id=1, source_target_pairs={{0,4},{1,5},{2,6},{3,7},{4,0},{5,1},{6,2},{7,3},{8,12},{9,13},{10,... | collective-permute-start | bytes 368648 | tf_op jit(solution)/shard_map/ppermute | solution.py:262
  12.5 5.0 %collective-permute-start.5 = (bf16[48,1280]{1,0:T(8,128)(2,1)S(1)}, bf16[48,1280]{1,0:T(8,128)(2,1)S(1)}, u32[]{:S(2)}, u32[]{:S(2)}) collective-permute-start(bf16[48,1280]{1,0:T(8,128)(2,1)S(1)} %get-tuple-element.14), channel_id=1, source_target_pairs={{0,2},{1,3},{2,0},{3,1},{4,6},{5,7},{6,4},{7,5},{8,10},{9,11},{10,... | collective-permute-start | bytes 368648 | tf_op jit(solution)/shard_map/ppermute | solution.py:262
  19.5 5.1 %collective-permute-start.6 = (bf16[8,1632]{1,0:T(8,128)(2,1)S(1)}, bf16[8,1632]{1,0:T(8,128)(2,1)S(1)}, u32[]{:S(2)}, u32[]{:S(2)}) collective-permute-start(bf16[8,1632]{1,0:T(8,128)(2,1)S(1)} %get-tuple-element.15), channel_id=1, source_target_pairs={{25,0},{24,1},{27,2},{26,3},{29,4},{28,5},{31,6},{30,7},{1,8},{0,9... | collective-permute-start | bytes 78344 | tf_op jit(solution)/shard_map/ppermute | solution.py:278
  19.6 5.1 %collective-permute-start.7 = (bf16[8,1632]{1,0:T(8,128)(2,1)S(1)}, bf16[8,1632]{1,0:T(8,128)(2,1)S(1)}, u32[]{:S(2)}, u32[]{:S(2)}) collective-permute-start(bf16[8,1632]{1,0:T(8,128)(2,1)S(1)} %get-tuple-element.16), channel_id=1, source_target_pairs={{9,0},{8,1},{11,2},{10,3},{13,4},{12,5},{15,6},{14,7},{17,8},{16,9... | collective-permute-start | bytes 78344 | tf_op jit(solution)/shard_map/ppermute | solution.py:278
where the time goes:
time: 25.5 us; the launch traced here: 25.3 us
  starting transfers between devices  12.7 us (50%)
  waiting for transfers between devices  8.15 us (32%)
  Pallas kernels  3.4 us (13%)
  local copies, waits for them, and re-layouts  1.04 us (4%)
    ppermute x4, waiting for transfers between devices, swapped(): return lax.ppermute(block, axis, [(k, k ^ m) for k in devices])  5.18 us
    ppermute x2, starting transfers between devices, passed_along(): return lax.ppermute(block, 'chan', route)  5.09 us
    ppermute x4, starting transfers between devices, swapped(): return lax.ppermute(block, axis, [(k, k ^ m) for k in devices])  4.01 us
    ppermute x2, starting transfers between devices, passed_across(): return lax.ppermute(block, ('chan', 'tm'), route)  3.59 us
    pallas_call x6, Pallas kernels, call(): pl.pallas_call(kernel, out_shape=out_shape, in_specs=[spec] * len(inputs)...  3.4 us
    ppermute x2, waiting for transfers between devices, passed_across(): return lax.ppermute(block, ('chan', 'tm'), route)  1.54 us
    ppermute x2, waiting for transfers between devices, passed_along(): return lax.ppermute(block, 'chan', route)  1.43 us
    unnamed x2, local copies, waits for them, and re-layouts  1.04 us
  transfers between devices with their start and end apart: 8, of which 7 were waited for; matrix products, arithmetic and copies ran while one was open for 0% of the time, Pallas kernels for 2%

commit v1 on v0

--- a/solution.py
+++ b/solution.py
@@ -12,7 +12,7 @@
 MAXLAG = 25
 W2 = 64
 LAGS = 51
-FINE = 4
+FINE = 8
 COARSE = -(-LAGS // FINE)
 LANES = 128
 PAD = 128
@@ -198,17 +198,14 @@
                 j * group : (j + 1) * group, first:last
             ]
         table[h * LANES : (h + 1) * LANES] = mixed[h].T.astype(table.dtype)
-    lane = lax.broadcasted_iota(jnp.int32, (sources, LANES), 1)
+    lane = lax.broadcasted_iota(jnp.int32, (sources, LANES), 1).astype(table.dtype)
     width = group * LAGS
     tiles = [None] * -(-width // LANES)
 
-    def place(tile, piece, low, high):
-        if tiles[tile] is None:
-            tiles[tile] = piece
-        elif low == 0:
-            tiles[tile] = jnp.where(lane < high, piece, tiles[tile])
-        else:
-            tiles[tile] = jnp.where(lane >= low, piece, tiles[tile])
+    def place(tile, piece, low):
+        if low and tiles[tile] is not None:
+            piece = jnp.where(lane >= low, piece, tiles[tile])
+        tiles[tile] = piece
 
     for b in range(group):
         column = b * FINE
@@ -223,7 +220,7 @@
                 piece = pltpu.roll(piece, shift, 1)
             count = min(FINE, LAGS - i * FINE)
             tile, low = start // LANES, start % LANES
-            place(tile, piece, low, LANES)
+            place(tile, piece, low)
             if low + count > LANES:
                 tiles[tile + 1] = piece
     for tile, value in enumerate(tiles):

time: 25.5 us -> 25 us (0.980)
  Pallas kernels: 3.4 us -> 2.97 us
    pallas_call x6, Pallas kernels: 3.4 us -> 2.97 us  [call(): pl.pallas_call(kernel, out_shape=out_shape, in_specs=[spec] * len(inputs)...]
where the time goes in v1:
time: 25 us; the launch traced here: 24.9 us
  starting transfers between devices  12.7 us (51%)
  waiting for transfers between devices  8.15 us (33%)
  Pallas kernels  2.97 us (12%)
  local copies, waits for them, and re-layouts  1.04 us (4%)
    ppermute x4, waiting for transfers between devices, swapped(): return lax.ppermute(block, axis, [(k, k ^ m) for k in devices])  5.18 us
    ppermute x2, starting transfers between devices, passed_along(): return lax.ppermute(block, 'chan', route)  5.09 us
    ppermute x4, starting transfers between devices, swapped(): return lax.ppermute(block, axis, [(k, k ^ m) for k in devices])  4.01 us
    ppermute x2, starting transfers between devices, passed_across(): return lax.ppermute(block, ('chan', 'tm'), route)  3.59 us
    pallas_call x6, Pallas kernels, call(): pl.pallas_call(kernel, out_shape=out_shape, in_specs=[spec] * len(inputs)...  2.97 us
    ppermute x2, waiting for transfers between devices, passed_across(): return lax.ppermute(block, ('chan', 'tm'), route)  1.54 us
    ppermute x2, waiting for transfers between devices, passed_along(): return lax.ppermute(block, 'chan', route)  1.43 us
    unnamed x2, local copies, waits for them, and re-layouts  1.04 us
  transfers between devices with their start and end apart: 8, of which 7 were waited for; matrix products, arithmetic and copies ran while one was open for 0% of the time, Pallas kernels for 2%

profile of v1, /device:TPU:0, one launch (start us, length us, event | category | flops | bytes accessed | tf_op | source)
XLA Modules:
  0.0 24.9 jit_solution(18050108487389020321)
XLA Ops:
  0.0 0.5 %collective-permute-start = (f32[256,512]{1,0:T(8,128)}, f32[256,512]{1,0:T(8,128)S(1)}, u32[]{:S(2)}, u32[]{:S(2)}) collective-permute-start(f32[256,512]{1,0:T(8,128)} %x_ref.1), channel_id=1, source_target_pairs={{0,1},{1,0},{2,3},{3,2},{4,5},{5,4},{6,7},{7,6},{8,9},{9,8},{10,11... | collective-permute-start | bytes 1572872 | tf_op jit(solution)/shard_map/ppermute | solution.py:259
  0.5 0.0 copy-start
  0.5 1.0 %copy-done = f32[256,512]{1,0:T(8,128)S(1)} copy-done((f32[256,512]{1,0:T(8,128)S(1)}, f32[256,512]{1,0:T(8,128)}, u32[]{:S(2)}) %copy-start) | copy-done | bytes 524312
  1.5 0.7 %collective-permute-done.other_ref = f32[256,512]{1,0:T(8,128)S(1)} collective-permute-done((f32[256,512]{1,0:T(8,128)}, f32[256,512]{1,0:T(8,128)S(1)}, u32[]{:S(2)}, u32[]{:S(2)}) %collective-permute-start) | collective-permute-done | bytes 524320 | tf_op jit(solution)/shard_map/ppermute | solution.py:259
  2.2 0.2 shard_map.19
  2.4 3.0 %collective-permute-start.2 = (bf16[8,1280]{1,0:T(8,128)(2,1)S(1)}, bf16[8,1280]{1,0:T(8,128)(2,1)S(1)}, u32[]{:S(2)}, u32[]{:S(2)}) collective-permute-start(bf16[8,1280]{1,0:T(8,128)(2,1)S(1)} %shard_map.19), channel_id=1, source_target_pairs={{24,0},{0,8},{8,16},{16,24},{25,1},{1,9},{9,17},{17,25},{26,2},{2,... | collective-permute-start | bytes 61448 | tf_op jit(solution)/shard_map/ppermute | solution.py:265
  5.4 2.1 %collective-permute-start.1 = (bf16[8,1280]{1,0:T(8,128)(2,1)S(1)}, bf16[8,1280]{1,0:T(8,128)(2,1)S(1)}, u32[]{:S(2)}, u32[]{:S(2)}) collective-permute-start(bf16[8,1280]{1,0:T(8,128)(2,1)S(1)} %shard_map.19), channel_id=1, source_target_pairs={{8,0},{16,8},{24,16},{0,24},{9,1},{17,9},{25,17},{1,25},{10,2},{18... | collective-permute-start | bytes 61448 | tf_op jit(solution)/shard_map/ppermute | solution.py:265
  7.5 0.5 %shard_map.18.receivers_ref = bf16[128,1280]{1,0:T(8,128)(2,1)S(1)} custom-call(f32[136,512]{1,0:T(8,128)S(1)} %shard_map.17.own_ref, f32[256,512]{1,0:T(8,128)S(1)} %collective-permute-done.other_ref), custom_call_target="tpu_custom_call" | custom-call | flops 536870912 | bytes 802816 | tf_op jit(solution)/shard_map/pallas_call | solution.py:244
  8.0 1.3 %collective-permute-done.2.refs_1_ = bf16[8,1280]{1,0:T(8,128)(2,1)S(1)} collective-permute-done((bf16[8,1280]{1,0:T(8,128)(2,1)S(1)}, bf16[8,1280]{1,0:T(8,128)(2,1)S(1)}, u32[]{:S(2)}, u32[]{:S(2)}) %collective-permute-start.2) | collective-permute-done | bytes 20512 | tf_op jit(solution)/shard_map/ppermute | solution.py:265
  9.3 0.1 collective-permute-done.1.refs_0_
  9.5 2.5 %collective-permute-start.3 = (bf16[48,1280]{1,0:T(8,128)(2,1)S(1)}, bf16[48,1280]{1,0:T(8,128)(2,1)S(1)}, u32[]{:S(2)}, u32[]{:S(2)}) collective-permute-start(bf16[48,1280]{1,0:T(8,128)(2,1)S(1)} %get-tuple-element.12), channel_id=1, source_target_pairs={{0,6},{1,7},{2,4},{3,5},{4,2},{5,3},{6,0},{7,1},{8,14},{9,15},{10,... | collective-permute-start | bytes 368648 | tf_op jit(solution)/shard_map/ppermute | solution.py:259
  12.0 0.5 %collective-permute-start.4 = (bf16[48,1280]{1,0:T(8,128)(2,1)S(1)}, bf16[48,1280]{1,0:T(8,128)(2,1)S(1)}, u32[]{:S(2)}, u32[]{:S(2)}) collective-permute-start(bf16[48,1280]{1,0:T(8,128)(2,1)S(1)} %get-tuple-element.13), channel_id=1, source_target_pairs={{0,4},{1,5},{2,6},{3,7},{4,0},{5,1},{6,2},{7,3},{8,12},{9,13},{10,... | collective-permute-start | bytes 368648 | tf_op jit(solution)/shard_map/ppermute | solution.py:259
  12.5 0.5 %collective-permute-start.5 = (bf16[48,1280]{1,0:T(8,128)(2,1)S(1)}, bf16[48,1280]{1,0:T(8,128)(2,1)S(1)}, u32[]{:S(2)}, u32[]{:S(2)}) collective-permute-start(bf16[48,1280]{1,0:T(8,128)(2,1)S(1)} %get-tuple-element.14), channel_id=1, source_target_pairs={{0,2},{1,3},{2,0},{3,1},{4,6},{5,7},{6,4},{7,5},{8,10},{9,11},{10,... | collective-permute-start | bytes 368648 | tf_op jit(solution)/shard_map/ppermute | solution.py:259
  13.0 3.1 %collective-permute-done.3.refs_1_ = bf16[48,1280]{1,0:T(8,128)(2,1)S(1)} collective-permute-done((bf16[48,1280]{1,0:T(8,128)(2,1)S(1)}, bf16[48,1280]{1,0:T(8,128)(2,1)S(1)}, u32[]{:S(2)}, u32[]{:S(2)}) %collective-permute-start.3) | collective-permute-done | bytes 122912 | tf_op jit(solution)/shard_map/ppermute | solution.py:259
  16.1 1.2 %collective-permute-done.4.refs_2_ = bf16[48,1280]{1,0:T(8,128)(2,1)S(1)} collective-permute-done((bf16[48,1280]{1,0:T(8,128)(2,1)S(1)}, bf16[48,1280]{1,0:T(8,128)(2,1)S(1)}, u32[]{:S(2)}, u32[]{:S(2)}) %collective-permute-start.4) | collective-permute-done | bytes 122912 | tf_op jit(solution)/shard_map/ppermute | solution.py:259
  17.3 0.2 collective-permute-done.5.refs_3_
  17.5 1.6 %shard_map.21 = (bf16[8,1632]{1,0:T(8,128)(2,1)S(1)}, bf16[8,1632]{1,0:T(8,128)(2,1)S(1)}) custom-call(bf16[48,1280]{1,0:T(8,128)(2,1)S(1)} %get-tuple-element.11.refs_0_, bf16[48,1280]{1,0:T(8,128)(2,1)S(1)} %collective-permute-done.3.refs_1_, bf16[48,1280]{1,0:T(8,128)(2,1)S(1)} %collective-permute-done.4.refs_2_, ...), custom_call_target="tpu_custom_call" | custom-call | flops 293601280 | bytes 491520 | tf_op jit(solution)/shard_map/pallas_call | solution.py:244
  19.1 0.1 collective-permute-start.6
  19.1 3.5 %collective-permute-start.7 = (bf16[8,1632]{1,0:T(8,128)(2,1)S(1)}, bf16[8,1632]{1,0:T(8,128)(2,1)S(1)}, u32[]{:S(2)}, u32[]{:S(2)}) collective-permute-start(bf16[8,1632]{1,0:T(8,128)(2,1)S(1)} %get-tuple-element.16), channel_id=1, source_target_pairs={{9,0},{8,1},{11,2},{10,3},{13,4},{12,5},{15,6},{14,7},{17,8},{16,9... | collective-permute-start | bytes 78344 | tf_op jit(solution)/shard_map/ppermute | solution.py:275
  22.7 1.5 %collective-permute-done.6.refs_0_ = bf16[8,1632]{1,0:T(8,128)(2,1)S(1)} collective-permute-done((bf16[8,1632]{1,0:T(8,128)(2,1)S(1)}, bf16[8,1632]{1,0:T(8,128)(2,1)S(1)}, u32[]{:S(2)}, u32[]{:S(2)}) %collective-permute-start.6) | collective-permute-done | bytes 26144 | tf_op jit(solution)/shard_map/ppermute | solution.py:275
  24.2 0.0 collective-permute-done.7.refs_1_
  24.2 0.7 %shard_map.22 = f32[8,2,1632]{2,1,0:T(2,128)} custom-call(bf16[8,1632]{1,0:T(8,128)(2,1)S(1)} %collective-permute-done.6.refs_0_, bf16[8,1632]{1,0:T(8,128)(2,1)S(1)} %collective-permute-done.7.refs_1_), custom_call_target="tpu_custom_call" | custom-call | bytes 52224 | tf_op jit(solution)/shard_map/pallas_call | solution.py:244
  (2 shorter events, 0.1 us)
Async XLA Ops:
  0.0 2.2 %collective-permute-start = (f32[256,512]{1,0:T(8,128)}, f32[256,512]{1,0:T(8,128)S(1)}, u32[]{:S(2)}, u32[]{:S(2)}) collective-permute-start(f32[256,512]{1,0:T(8,128)} %x_ref.1), channel_id=1, source_target_pairs={{0,1},{1,0},{2,3},{3,2},{4,5},{5,4},{6,7},{7,6},{8,9},{9,8},{10,11... | collective-permute-start | bytes 1572872 | tf_op jit(solution)/shard_map/ppermute | solution.py:259
  0.5 1.0 %copy-start = (f32[256,512]{1,0:T(8,128)S(1)}, f32[256,512]{1,0:T(8,128)}, u32[]{:S(2)}) copy-start(f32[256,512]{1,0:T(8,128)} %x_ref.1) | copy-start | bytes 1572868
  2.4 6.9 %collective-permute-start.2 = (bf16[8,1280]{1,0:T(8,128)(2,1)S(1)}, bf16[8,1280]{1,0:T(8,128)(2,1)S(1)}, u32[]{:S(2)}, u32[]{:S(2)}) collective-permute-start(bf16[8,1280]{1,0:T(8,128)(2,1)S(1)} %shard_map.19), channel_id=1, source_target_pairs={{24,0},{0,8},{8,16},{16,24},{25,1},{1,9},{9,17},{17,25},{26,2},{2,... | collective-permute-start | bytes 61448 | tf_op jit(solution)/shard_map/ppermute | solution.py:265
  5.4 4.0 %collective-permute-start.1 = (bf16[8,1280]{1,0:T(8,128)(2,1)S(1)}, bf16[8,1280]{1,0:T(8,128)(2,1)S(1)}, u32[]{:S(2)}, u32[]{:S(2)}) collective-permute-start(bf16[8,1280]{1,0:T(8,128)(2,1)S(1)} %shard_map.19), channel_id=1, source_target_pairs={{8,0},{16,8},{24,16},{0,24},{9,1},{17,9},{25,17},{1,25},{10,2},{18... | collective-permute-start | bytes 61448 | tf_op jit(solution)/shard_map/ppermute | solution.py:265
  9.5 6.7 %collective-permute-start.3 = (bf16[48,1280]{1,0:T(8,128)(2,1)S(1)}, bf16[48,1280]{1,0:T(8,128)(2,1)S(1)}, u32[]{:S(2)}, u32[]{:S(2)}) collective-permute-start(bf16[48,1280]{1,0:T(8,128)(2,1)S(1)} %get-tuple-element.12), channel_id=1, source_target_pairs={{0,6},{1,7},{2,4},{3,5},{4,2},{5,3},{6,0},{7,1},{8,14},{9,15},{10,... | collective-permute-start | bytes 368648 | tf_op jit(solution)/shard_map/ppermute | solution.py:259
  12.0 5.4 %collective-permute-start.4 = (bf16[48,1280]{1,0:T(8,128)(2,1)S(1)}, bf16[48,1280]{1,0:T(8,128)(2,1)S(1)}, u32[]{:S(2)}, u32[]{:S(2)}) collective-permute-start(bf16[48,1280]{1,0:T(8,128)(2,1)S(1)} %get-tuple-element.13), channel_id=1, source_target_pairs={{0,4},{1,5},{2,6},{3,7},{4,0},{5,1},{6,2},{7,3},{8,12},{9,13},{10,... | collective-permute-start | bytes 368648 | tf_op jit(solution)/shard_map/ppermute | solution.py:259
  12.5 5.0 %collective-permute-start.5 = (bf16[48,1280]{1,0:T(8,128)(2,1)S(1)}, bf16[48,1280]{1,0:T(8,128)(2,1)S(1)}, u32[]{:S(2)}, u32[]{:S(2)}) collective-permute-start(bf16[48,1280]{1,0:T(8,128)(2,1)S(1)} %get-tuple-element.14), channel_id=1, source_target_pairs={{0,2},{1,3},{2,0},{3,1},{4,6},{5,7},{6,4},{7,5},{8,10},{9,11},{10,... | collective-permute-start | bytes 368648 | tf_op jit(solution)/shard_map/ppermute | solution.py:259
  19.1 5.1 %collective-permute-start.6 = (bf16[8,1632]{1,0:T(8,128)(2,1)S(1)}, bf16[8,1632]{1,0:T(8,128)(2,1)S(1)}, u32[]{:S(2)}, u32[]{:S(2)}) collective-permute-start(bf16[8,1632]{1,0:T(8,128)(2,1)S(1)} %get-tuple-element.15), channel_id=1, source_target_pairs={{25,0},{24,1},{27,2},{26,3},{29,4},{28,5},{31,6},{30,7},{1,8},{0,9... | collective-permute-start | bytes 78344 | tf_op jit(solution)/shard_map/ppermute | solution.py:275
  19.1 5.1 %collective-permute-start.7 = (bf16[8,1632]{1,0:T(8,128)(2,1)S(1)}, bf16[8,1632]{1,0:T(8,128)(2,1)S(1)}, u32[]{:S(2)}, u32[]{:S(2)}) collective-permute-start(bf16[8,1632]{1,0:T(8,128)(2,1)S(1)} %get-tuple-element.16), channel_id=1, source_target_pairs={{9,0},{8,1},{11,2},{10,3},{13,4},{12,5},{15,6},{14,7},{17,8},{16,9... | collective-permute-start | bytes 78344 | tf_op jit(solution)/shard_map/ppermute | solution.py:275

commit v2 on v1

--- a/solution.py
+++ b/solution.py
@@ -15,7 +15,6 @@
 FINE = 8
 COARSE = -(-LAGS // FINE)
 LANES = 128
-PAD = 128
 CORES = 2
 
 
@@ -156,17 +155,39 @@
         v * l / (l + a / (2 * W2 + 1)) for v, l, a in zip(values, levels, added)
     ]
     shard = length // CORES
-    padding = jnp.zeros((height, PAD), held.dtype)
     for k in range(chips * CORES):
         c, part = k // CORES, k % CORES
-        pieces = [held[c, :, part * shard : (part + 1) * shard], padding]
+        pieces = [held[c, :, part * shard : (part + 1) * shard]]
         if part == 0:
             head = jnp.where(left, ends[c], lanes(c, 0)).astype(held.dtype)
-            pieces = [head, held[c, :, LANES:shard], padding]
+            pieces = [head, held[c, :, LANES:shard]]
         if part == CORES - 1:
             last = jnp.where(left, lanes(c, tail), ends[c + 1]).astype(held.dtype)
-            pieces = [held[c, :, part * shard : tail], last, padding]
+            pieces = [held[c, :, part * shard : tail], last]
         yield jnp.concatenate(pieces, axis=1)
+
+
+def lane_numbers(rows, dtype):
+    return lax.broadcasted_iota(jnp.int32, (rows, LANES), 1).astype(dtype)
+
+
+def shifted(rows, shift):
+    height, length = rows.shape
+    nothing = jnp.zeros((height, LANES), rows.dtype)
+    if not shift:
+        return jnp.concatenate([rows, nothing], axis=1)
+    turned = [
+        pltpu.roll(rows[:, first : first + LANES], shift, 1)
+        for first in range(0, length, LANES)
+    ]
+    behind = lane_numbers(height, rows.dtype) >= shift
+    return jnp.concatenate(
+        [
+            jnp.where(behind, here, before)
+            for before, here in zip([nothing] + turned, turned + [nothing])
+        ],
+        axis=1,
+    )
 
 
 def correlate_kernel(offsets, scale, *refs):
@@ -179,10 +200,8 @@
     product = None
     for wide in finished_shards(runs, held):
         receivers, senders = wide[:group], wide[group:]
-        fine = [pltpu.roll(receivers, MAXLAG - j, 1) for j in range(FINE)]
-        coarse = [
-            pltpu.roll(senders, FINE * i, 1) if i else senders for i in range(COARSE)
-        ]
+        fine = [shifted(receivers, MAXLAG - j) for j in range(FINE)]
+        coarse = [shifted(senders, FINE * i) for i in range(COARSE)]
         term = lax.dot_general(
             jnp.concatenate(fine, axis=0).astype(jnp.bfloat16),
             jnp.concatenate(coarse, axis=0).astype(jnp.bfloat16),
@@ -198,32 +217,34 @@
                 j * group : (j + 1) * group, first:last
             ]
         table[h * LANES : (h + 1) * LANES] = mixed[h].T.astype(table.dtype)
-    lane = lax.broadcasted_iota(jnp.int32, (sources, LANES), 1).astype(table.dtype)
+    columns = table.shape[1]
+    turned = []
+    for i in range(COARSE):
+        block = table[i * sources : (i + 1) * sources]
+        turned.append(pltpu.roll(block, FINE * i, 1) if i else block)
+    lane = lane_numbers(sources, table.dtype)
     width = group * LAGS
-    tiles = [None] * -(-width // LANES)
-
-    def place(tile, piece, low):
-        if low and tiles[tile] is not None:
+
+    def place(tiles, tile, piece, low):
+        if low and tile in tiles:
             piece = jnp.where(lane >= low, piece, tiles[tile])
         tiles[tile] = piece
 
+    tiles = {}
     for b in range(group):
-        column = b * FINE
+        joined = {}
         for i in range(COARSE):
-            piece = table[
-                i * sources : (i + 1) * sources,
-                column // LANES * LANES : (column // LANES + 1) * LANES,
-            ]
-            start = b * LAGS + i * FINE
-            shift = (start - column) % LANES
-            if shift:
-                piece = pltpu.roll(piece, shift, 1)
-            count = min(FINE, LAGS - i * FINE)
-            tile, low = start // LANES, start % LANES
-            place(tile, piece, low)
-            if low + count > LANES:
-                tiles[tile + 1] = piece
-    for tile, value in enumerate(tiles):
+            tile, low = divmod((b + i) * FINE % columns, LANES)
+            piece = turned[i][:, tile * LANES : (tile + 1) * LANES]
+            place(joined, tile, piece, low)
+        turn = b * (LAGS - FINE) % LANES
+        if turn:
+            joined = {tile: pltpu.roll(v, turn, 1) for tile, v in joined.items()}
+        for lag in range(LAGS):
+            at, to = (b * FINE + lag) % columns, b * LAGS + lag
+            if lag == 0 or at % LANES == 0 or to % LANES == 0:
+                place(tiles, to // LANES, joined[at // LANES], to % LANES)
+    for tile, value in tiles.items():
         first = tile * LANES
         last = min(first + LANES, width)
         for o in range(offsets):
@@ -327,7 +348,7 @@
             pltpu.VMEM((heights // LANES, columns, LANES), jnp.float32),
             pltpu.VMEM((heights, columns), kind),
         ],
-        flops=2 * shards * (length + PAD) * group * FINE * COARSE * sources,
+        flops=2 * shards * (length + LANES) * group * FINE * COARSE * sources,
     )
     arrived = [passed_across(r, -d) for r, d in zip(results, steps)]
     return call(

time: 25 us -> 24.9 us (level)
  no operation moved by 1% of the time
where the time goes in v2:
time: 24.9 us; the launch traced here: 24.8 us
  starting transfers between devices  12.7 us (51%)
  waiting for transfers between devices  8.15 us (33%)
  Pallas kernels  2.84 us (11%)
  local copies, waits for them, and re-layouts  1.04 us (4%)
    ppermute x4, waiting for transfers between devices, swapped(): return lax.ppermute(block, axis, [(k, k ^ m) for k in devices])  5.18 us
    ppermute x2, starting transfers between devices, passed_along(): return lax.ppermute(block, 'chan', route)  5.09 us
    ppermute x4, starting transfers between devices, swapped(): return lax.ppermute(block, axis, [(k, k ^ m) for k in devices])  4.01 us
    ppermute x2, starting transfers between devices, passed_across(): return lax.ppermute(block, ('chan', 'tm'), route)  3.59 us
    pallas_call x6, Pallas kernels, call(): pl.pallas_call(kernel, out_shape=out_shape, in_specs=[spec] * len(inputs)...  2.84 us
    ppermute x2, waiting for transfers between devices, passed_across(): return lax.ppermute(block, ('chan', 'tm'), route)  1.54 us
    ppermute x2, waiting for transfers between devices, passed_along(): return lax.ppermute(block, 'chan', route)  1.43 us
    unnamed x2, local copies, waits for them, and re-layouts  1.04 us
  transfers between devices with their start and end apart: 8, of which 7 were waited for; matrix products, arithmetic and copies ran while one was open for 0% of the time, Pallas kernels for 2%

profile of v2, /device:TPU:0, one launch (start us, length us, event | category | flops | bytes accessed | tf_op | source)
XLA Modules:
  0.0 24.8 jit_solution(9971610601780536448)
XLA Ops:
  0.0 0.5 %collective-permute-start = (f32[256,512]{1,0:T(8,128)}, f32[256,512]{1,0:T(8,128)S(1)}, u32[]{:S(2)}, u32[]{:S(2)}) collective-permute-start(f32[256,512]{1,0:T(8,128)} %x_ref.1), channel_id=1, source_target_pairs={{0,1},{1,0},{2,3},{3,2},{4,5},{5,4},{6,7},{7,6},{8,9},{9,8},{10,11... | collective-permute-start | bytes 1572872 | tf_op jit(solution)/shard_map/ppermute | solution.py:280
  0.5 0.0 copy-start
  0.5 1.0 %copy-done = f32[256,512]{1,0:T(8,128)S(1)} copy-done((f32[256,512]{1,0:T(8,128)S(1)}, f32[256,512]{1,0:T(8,128)}, u32[]{:S(2)}) %copy-start) | copy-done | bytes 524312
  1.5 0.7 %collective-permute-done.other_ref = f32[256,512]{1,0:T(8,128)S(1)} collective-permute-done((f32[256,512]{1,0:T(8,128)}, f32[256,512]{1,0:T(8,128)S(1)}, u32[]{:S(2)}, u32[]{:S(2)}) %collective-permute-start) | collective-permute-done | bytes 524320 | tf_op jit(solution)/shard_map/ppermute | solution.py:280
  2.2 0.2 shard_map.19
  2.4 3.0 %collective-permute-start.2 = (bf16[8,1280]{1,0:T(8,128)(2,1)S(1)}, bf16[8,1280]{1,0:T(8,128)(2,1)S(1)}, u32[]{:S(2)}, u32[]{:S(2)}) collective-permute-start(bf16[8,1280]{1,0:T(8,128)(2,1)S(1)} %shard_map.19), channel_id=1, source_target_pairs={{24,0},{0,8},{8,16},{16,24},{25,1},{1,9},{9,17},{17,25},{26,2},{2,... | collective-permute-start | bytes 61448 | tf_op jit(solution)/shard_map/ppermute | solution.py:286
  5.4 2.1 %collective-permute-start.1 = (bf16[8,1280]{1,0:T(8,128)(2,1)S(1)}, bf16[8,1280]{1,0:T(8,128)(2,1)S(1)}, u32[]{:S(2)}, u32[]{:S(2)}) collective-permute-start(bf16[8,1280]{1,0:T(8,128)(2,1)S(1)} %shard_map.19), channel_id=1, source_target_pairs={{8,0},{16,8},{24,16},{0,24},{9,1},{17,9},{25,17},{1,25},{10,2},{18... | collective-permute-start | bytes 61448 | tf_op jit(solution)/shard_map/ppermute | solution.py:286
  7.5 0.5 %shard_map.18.receivers_ref = bf16[128,1280]{1,0:T(8,128)(2,1)S(1)} custom-call(f32[136,512]{1,0:T(8,128)S(1)} %shard_map.17.own_ref, f32[256,512]{1,0:T(8,128)S(1)} %collective-permute-done.other_ref), custom_call_target="tpu_custom_call" | custom-call | flops 536870912 | bytes 802816 | tf_op jit(solution)/shard_map/pallas_call | solution.py:265
  8.0 1.3 %collective-permute-done.2.refs_1_ = bf16[8,1280]{1,0:T(8,128)(2,1)S(1)} collective-permute-done((bf16[8,1280]{1,0:T(8,128)(2,1)S(1)}, bf16[8,1280]{1,0:T(8,128)(2,1)S(1)}, u32[]{:S(2)}, u32[]{:S(2)}) %collective-permute-start.2) | collective-permute-done | bytes 20512 | tf_op jit(solution)/shard_map/ppermute | solution.py:286
  9.3 0.1 collective-permute-done.1.refs_0_
  9.5 2.5 %collective-permute-start.3 = (bf16[48,1280]{1,0:T(8,128)(2,1)S(1)}, bf16[48,1280]{1,0:T(8,128)(2,1)S(1)}, u32[]{:S(2)}, u32[]{:S(2)}) collective-permute-start(bf16[48,1280]{1,0:T(8,128)(2,1)S(1)} %get-tuple-element.12), channel_id=1, source_target_pairs={{0,6},{1,7},{2,4},{3,5},{4,2},{5,3},{6,0},{7,1},{8,14},{9,15},{10,... | collective-permute-start | bytes 368648 | tf_op jit(solution)/shard_map/ppermute | solution.py:280
  12.0 0.5 %collective-permute-start.4 = (bf16[48,1280]{1,0:T(8,128)(2,1)S(1)}, bf16[48,1280]{1,0:T(8,128)(2,1)S(1)}, u32[]{:S(2)}, u32[]{:S(2)}) collective-permute-start(bf16[48,1280]{1,0:T(8,128)(2,1)S(1)} %get-tuple-element.13), channel_id=1, source_target_pairs={{0,4},{1,5},{2,6},{3,7},{4,0},{5,1},{6,2},{7,3},{8,12},{9,13},{10,... | collective-permute-start | bytes 368648 | tf_op jit(solution)/shard_map/ppermute | solution.py:280
  12.5 0.5 %collective-permute-start.5 = (bf16[48,1280]{1,0:T(8,128)(2,1)S(1)}, bf16[48,1280]{1,0:T(8,128)(2,1)S(1)}, u32[]{:S(2)}, u32[]{:S(2)}) collective-permute-start(bf16[48,1280]{1,0:T(8,128)(2,1)S(1)} %get-tuple-element.14), channel_id=1, source_target_pairs={{0,2},{1,3},{2,0},{3,1},{4,6},{5,7},{6,4},{7,5},{8,10},{9,11},{10,... | collective-permute-start | bytes 368648 | tf_op jit(solution)/shard_map/ppermute | solution.py:280
  13.0 3.1 %collective-permute-done.3.refs_1_ = bf16[48,1280]{1,0:T(8,128)(2,1)S(1)} collective-permute-done((bf16[48,1280]{1,0:T(8,128)(2,1)S(1)}, bf16[48,1280]{1,0:T(8,128)(2,1)S(1)}, u32[]{:S(2)}, u32[]{:S(2)}) %collective-permute-start.3) | collective-permute-done | bytes 122912 | tf_op jit(solution)/shard_map/ppermute | solution.py:280
  16.1 1.2 %collective-permute-done.4.refs_2_ = bf16[48,1280]{1,0:T(8,128)(2,1)S(1)} collective-permute-done((bf16[48,1280]{1,0:T(8,128)(2,1)S(1)}, bf16[48,1280]{1,0:T(8,128)(2,1)S(1)}, u32[]{:S(2)}, u32[]{:S(2)}) %collective-permute-start.4) | collective-permute-done | bytes 122912 | tf_op jit(solution)/shard_map/ppermute | solution.py:280
  17.3 0.2 collective-permute-done.5.refs_3_
  17.5 1.4 %shard_map.21 = (bf16[8,1632]{1,0:T(8,128)(2,1)S(1)}, bf16[8,1632]{1,0:T(8,128)(2,1)S(1)}) custom-call(bf16[48,1280]{1,0:T(8,128)(2,1)S(1)} %get-tuple-element.11.refs_0_, bf16[48,1280]{1,0:T(8,128)(2,1)S(1)} %collective-permute-done.3.refs_1_, bf16[48,1280]{1,0:T(8,128)(2,1)S(1)} %collective-permute-done.4.refs_2_, ...), custom_call_target="tpu_custom_call" | custom-call | flops 293601280 | bytes 491520 | tf_op jit(solution)/shard_map/pallas_call | solution.py:265
  18.9 0.1 collective-permute-start.6
  19.0 3.5 %collective-permute-start.7 = (bf16[8,1632]{1,0:T(8,128)(2,1)S(1)}, bf16[8,1632]{1,0:T(8,128)(2,1)S(1)}, u32[]{:S(2)}, u32[]{:S(2)}) collective-permute-start(bf16[8,1632]{1,0:T(8,128)(2,1)S(1)} %get-tuple-element.16), channel_id=1, source_target_pairs={{9,0},{8,1},{11,2},{10,3},{13,4},{12,5},{15,6},{14,7},{17,8},{16,9... | collective-permute-start | bytes 78344 | tf_op jit(solution)/shard_map/ppermute | solution.py:296
  22.5 1.5 %collective-permute-done.6.refs_0_ = bf16[8,1632]{1,0:T(8,128)(2,1)S(1)} collective-permute-done((bf16[8,1632]{1,0:T(8,128)(2,1)S(1)}, bf16[8,1632]{1,0:T(8,128)(2,1)S(1)}, u32[]{:S(2)}, u32[]{:S(2)}) %collective-permute-start.6) | collective-permute-done | bytes 26144 | tf_op jit(solution)/shard_map/ppermute | solution.py:296
  24.1 0.0 collective-permute-done.7.refs_1_
  24.1 0.7 %shard_map.22 = f32[8,2,1632]{2,1,0:T(2,128)} custom-call(bf16[8,1632]{1,0:T(8,128)(2,1)S(1)} %collective-permute-done.6.refs_0_, bf16[8,1632]{1,0:T(8,128)(2,1)S(1)} %collective-permute-done.7.refs_1_), custom_call_target="tpu_custom_call" | custom-call | bytes 52224 | tf_op jit(solution)/shard_map/pallas_call | solution.py:265
  (2 shorter events, 0.1 us)
Async XLA Ops:
  0.0 2.2 %collective-permute-start = (f32[256,512]{1,0:T(8,128)}, f32[256,512]{1,0:T(8,128)S(1)}, u32[]{:S(2)}, u32[]{:S(2)}) collective-permute-start(f32[256,512]{1,0:T(8,128)} %x_ref.1), channel_id=1, source_target_pairs={{0,1},{1,0},{2,3},{3,2},{4,5},{5,4},{6,7},{7,6},{8,9},{9,8},{10,11... | collective-permute-start | bytes 1572872 | tf_op jit(solution)/shard_map/ppermute | solution.py:280
  0.5 1.0 %copy-start = (f32[256,512]{1,0:T(8,128)S(1)}, f32[256,512]{1,0:T(8,128)}, u32[]{:S(2)}) copy-start(f32[256,512]{1,0:T(8,128)} %x_ref.1) | copy-start | bytes 1572868
  2.4 6.9 %collective-permute-start.2 = (bf16[8,1280]{1,0:T(8,128)(2,1)S(1)}, bf16[8,1280]{1,0:T(8,128)(2,1)S(1)}, u32[]{:S(2)}, u32[]{:S(2)}) collective-permute-start(bf16[8,1280]{1,0:T(8,128)(2,1)S(1)} %shard_map.19), channel_id=1, source_target_pairs={{24,0},{0,8},{8,16},{16,24},{25,1},{1,9},{9,17},{17,25},{26,2},{2,... | collective-permute-start | bytes 61448 | tf_op jit(solution)/shard_map/ppermute | solution.py:286
  5.4 4.0 %collective-permute-start.1 = (bf16[8,1280]{1,0:T(8,128)(2,1)S(1)}, bf16[8,1280]{1,0:T(8,128)(2,1)S(1)}, u32[]{:S(2)}, u32[]{:S(2)}) collective-permute-start(bf16[8,1280]{1,0:T(8,128)(2,1)S(1)} %shard_map.19), channel_id=1, source_target_pairs={{8,0},{16,8},{24,16},{0,24},{9,1},{17,9},{25,17},{1,25},{10,2},{18... | collective-permute-start | bytes 61448 | tf_op jit(solution)/shard_map/ppermute | solution.py:286
  9.5 6.7 %collective-permute-start.3 = (bf16[48,1280]{1,0:T(8,128)(2,1)S(1)}, bf16[48,1280]{1,0:T(8,128)(2,1)S(1)}, u32[]{:S(2)}, u32[]{:S(2)}) collective-permute-start(bf16[48,1280]{1,0:T(8,128)(2,1)S(1)} %get-tuple-element.12), channel_id=1, source_target_pairs={{0,6},{1,7},{2,4},{3,5},{4,2},{5,3},{6,0},{7,1},{8,14},{9,15},{10,... | collective-permute-start | bytes 368648 | tf_op jit(solution)/shard_map/ppermute | solution.py:280
  12.0 5.4 %collective-permute-start.4 = (bf16[48,1280]{1,0:T(8,128)(2,1)S(1)}, bf16[48,1280]{1,0:T(8,128)(2,1)S(1)}, u32[]{:S(2)}, u32[]{:S(2)}) collective-permute-start(bf16[48,1280]{1,0:T(8,128)(2,1)S(1)} %get-tuple-element.13), channel_id=1, source_target_pairs={{0,4},{1,5},{2,6},{3,7},{4,0},{5,1},{6,2},{7,3},{8,12},{9,13},{10,... | collective-permute-start | bytes 368648 | tf_op jit(solution)/shard_map/ppermute | solution.py:280
  12.5 5.0 %collective-permute-start.5 = (bf16[48,1280]{1,0:T(8,128)(2,1)S(1)}, bf16[48,1280]{1,0:T(8,128)(2,1)S(1)}, u32[]{:S(2)}, u32[]{:S(2)}) collective-permute-start(bf16[48,1280]{1,0:T(8,128)(2,1)S(1)} %get-tuple-element.14), channel_id=1, source_target_pairs={{0,2},{1,3},{2,0},{3,1},{4,6},{5,7},{6,4},{7,5},{8,10},{9,11},{10,... | collective-permute-start | bytes 368648 | tf_op jit(solution)/shard_map/ppermute | solution.py:280
  18.9 5.1 %collective-permute-start.6 = (bf16[8,1632]{1,0:T(8,128)(2,1)S(1)}, bf16[8,1632]{1,0:T(8,128)(2,1)S(1)}, u32[]{:S(2)}, u32[]{:S(2)}) collective-permute-start(bf16[8,1632]{1,0:T(8,128)(2,1)S(1)} %get-tuple-element.15), channel_id=1, source_target_pairs={{25,0},{24,1},{27,2},{26,3},{29,4},{28,5},{31,6},{30,7},{1,8},{0,9... | collective-permute-start | bytes 78344 | tf_op jit(solution)/shard_map/ppermute | solution.py:296
  19.0 5.1 %collective-permute-start.7 = (bf16[8,1632]{1,0:T(8,128)(2,1)S(1)}, bf16[8,1632]{1,0:T(8,128)(2,1)S(1)}, u32[]{:S(2)}, u32[]{:S(2)}) collective-permute-start(bf16[8,1632]{1,0:T(8,128)(2,1)S(1)} %get-tuple-element.16), channel_id=1, source_target_pairs={{9,0},{8,1},{11,2},{10,3},{13,4},{12,5},{15,6},{14,7},{17,8},{16,9... | collective-permute-start | bytes 78344 | tf_op jit(solution)/shard_map/ppermute | solution.py:296

commit v3 on v2

--- a/solution.py
+++ b/solution.py
@@ -63,7 +63,7 @@
     out_ref[...] = rows_for_here(x_ref, group, chips)
 
 
-def coded_rows(own, other):
+def coded_rows(own, other, exact):
     first_core = lax.rem(lax.axis_index("tm"), CORES) == 0
     x = jnp.concatenate(
         [jnp.where(first_core, own, other), jnp.where(first_core, other, own)], axis=1
@@ -91,20 +91,21 @@
     tail = length - LANES
     ends = jnp.where(left, normed[:, :LANES], normed[:, tail:])
     end_levels = jnp.where(left, levels[:, :LANES], levels[:, tail:])
-    coded = jnp.concatenate([normed, halves(ends)[1], end_levels], axis=1)
+    errors = [halves(ends)[1]] if exact else []
+    coded = jnp.concatenate([normed, end_levels] + errors, axis=1)
     return coded.astype(jnp.bfloat16)
 
 
 def code_sources_kernel(group, chips, own_ref, other_ref, out_ref):
     first = chips * group
     other = rows_for_here(other_ref, group, chips)
-    out_ref[...] = coded_rows(own_ref[first:], other[first:])
+    out_ref[...] = coded_rows(own_ref[first:], other[first:], True)
 
 
 def code_receivers_kernel(group, chips, own_ref, other_ref, out_ref):
     last = chips * group
     other = rows_for_here(other_ref, group, chips)
-    out_ref[...] = coded_rows(own_ref[:last], other[:last])
+    out_ref[...] = coded_rows(own_ref[:last], other[:last], False)
 
 
 def join_kernel(offsets, receivers_ref, *refs):
@@ -112,28 +113,39 @@
     group = receivers_ref.shape[0] // len(blocks)
     sources = [ref[...].astype(jnp.float32) for ref in given]
     receivers = receivers_ref[...].astype(jnp.float32)
+    sources = jnp.concatenate(sources, axis=0)
+    width = receivers.shape[1]
     for m, block in enumerate(blocks):
-        rows = [receivers[m * group : (m + 1) * group]] + sources
-        block[...] = jnp.concatenate(rows, axis=0).astype(jnp.bfloat16)
-
-
-def finished_shards(runs, held):
-    chips, height, width = held.shape
-    length = width - 2 * LANES
+        rows = jnp.concatenate(
+            [receivers[m * group : (m + 1) * group], sources[:, :width]], axis=0
+        )
+        pieces = [rows[:, first : first + LANES] for first in range(0, width, LANES)]
+        pieces.append(sources[:, width:])
+        block[...] = jnp.concatenate(pieces, axis=0).astype(jnp.bfloat16)
+
+
+def finished_shards(runs, held, sources, tiles):
+    chips, depth, _ = held.shape
+    height = (depth - sources) // (tiles + 1)
     chip = lax.div(lax.axis_index("tm"), CORES)
     for m in range(chips):
         held[chip ^ m] = runs[m]
     left = lax.broadcasted_iota(jnp.int32, (height, LANES), 1) < W2
-    tail = length - LANES
+
+    def tile(c, t):
+        return held[c, t * height : (t + 1) * height]
+
     end_values, end_levels = [], []
-
-    def lanes(c, first):
-        return held[c, :, first : first + LANES].astype(jnp.float32)
-
     for c in range(chips):
-        high = jnp.where(left, lanes(c, 0), lanes(c, tail))
-        end_values.append(high + lanes(c, length))
-        end_levels.append(lanes(c, length + LANES))
+        high = jnp.where(
+            left, tile(c, 0).astype(jnp.float32), tile(c, tiles - 1).astype(jnp.float32)
+        )
+        errors = held[c, (tiles + 1) * height :].astype(jnp.float32)
+        first = height - sources
+        end_values.append(
+            jnp.concatenate([high[:first], high[first:] + errors], axis=0)
+        )
+        end_levels.append(tile(c, tiles).astype(jnp.float32))
 
     def meeting(ends, outside):
         outside = [jnp.full((height, LANES), outside, jnp.float32)]
@@ -154,17 +166,14 @@
     ends = [
         v * l / (l + a / (2 * W2 + 1)) for v, l, a in zip(values, levels, added)
     ]
-    shard = length // CORES
-    for k in range(chips * CORES):
-        c, part = k // CORES, k % CORES
-        pieces = [held[c, :, part * shard : (part + 1) * shard]]
-        if part == 0:
-            head = jnp.where(left, ends[c], lanes(c, 0)).astype(held.dtype)
-            pieces = [head, held[c, :, LANES:shard]]
-        if part == CORES - 1:
-            last = jnp.where(left, lanes(c, tail), ends[c + 1]).astype(held.dtype)
-            pieces = [held[c, :, part * shard : tail], last]
-        yield jnp.concatenate(pieces, axis=1)
+    for c in range(chips):
+        row = [tile(c, t) for t in range(tiles)]
+        head = jnp.where(left, ends[c], row[0].astype(jnp.float32))
+        last = jnp.where(left, row[-1].astype(jnp.float32), ends[c + 1])
+        row = [head.astype(held.dtype)] + row[1:-1] + [last.astype(held.dtype)]
+        shard = tiles // CORES
+        for first in range(0, tiles, shard):
+            yield jnp.concatenate(row[first : first + shard], axis=1)
 
 
 def lane_numbers(rows, dtype):
@@ -190,15 +199,14 @@
     )
 
 
-def correlate_kernel(offsets, scale, *refs):
+def correlate_kernel(offsets, group, tiles, scale, *refs):
     chips = len(refs) - offsets - 3
     blocks, refs = refs[:chips], refs[chips:]
     outs, (held, mixed, table) = refs[:offsets], refs[offsets:]
     sources = offsets * SRC
-    group = held.shape[1] - sources
     runs = [ref[...].astype(held.dtype) for ref in blocks[:1] + blocks[:0:-1]]
     product = None
-    for wide in finished_shards(runs, held):
+    for wide in finished_shards(runs, held, sources, tiles):
         receivers, senders = wide[:group], wide[group:]
         fine = [shifted(receivers, MAXLAG - j) for j in range(FINE)]
         coarse = [shifted(senders, FINE * i) for i in range(COARSE)]
@@ -307,7 +315,8 @@
     sources = offsets * SRC
     scale = 1.0 / math.sqrt(length * shards)
     run = CORES * length
-    coded = run + 2 * LANES
+    tiles = run // LANES
+    depth = (group + sources) * (tiles + 1) + sources
 
     other = swapped(strain_rate, "tm", 1)
     own = call(
@@ -318,19 +327,19 @@
     )
     own_sources = call(
         functools.partial(code_sources_kernel, group, chips),
-        jax.ShapeDtypeStruct((SRC, coded), jnp.bfloat16),
+        jax.ShapeDtypeStruct((SRC, run + 2 * LANES), jnp.bfloat16),
         [own, other],
     )
     arrived = [passed_along(own_sources, d) for d in steps]
     own_receivers = call(
         functools.partial(code_receivers_kernel, group, chips),
-        jax.ShapeDtypeStruct((chips * group, coded), jnp.bfloat16),
+        jax.ShapeDtypeStruct((chips * group, run + LANES), jnp.bfloat16),
         [own, other],
         flops=8 * chips * group * run * (256 + 2 * LANES),
     )
     blocks = call(
         functools.partial(join_kernel, offsets),
-        [jax.ShapeDtypeStruct((group + sources, coded), jnp.bfloat16)] * chips,
+        [jax.ShapeDtypeStruct((depth, LANES), jnp.bfloat16)] * chips,
         [own_receivers] + arrived,
     )
     blocks = list(blocks[:1]) + [
@@ -340,11 +349,11 @@
     heights = -(-COARSE * sources // LANES) * LANES
     kind = jnp.float32 if group % 16 or sources % 16 else jnp.bfloat16
     results = call(
-        functools.partial(correlate_kernel, offsets, scale),
+        functools.partial(correlate_kernel, offsets, group, tiles, scale),
         [jax.ShapeDtypeStruct((SRC, group * LAGS), jnp.bfloat16)] * offsets,
         blocks,
         scratch=[
-            pltpu.VMEM((chips, group + sources, coded), kind),
+            pltpu.VMEM((chips, depth, LANES), kind),
             pltpu.VMEM((heights // LANES, columns, LANES), jnp.float32),
             pltpu.VMEM((heights, columns), kind),
         ],

time: 24.9 us -> 24.8 us (level)
  no operation moved by 1% of the time
where the time goes in v3:
time: 24.8 us; the launch traced here: 24.6 us
  starting transfers between devices  12.7 us (51%)
  waiting for transfers between devices  8.01 us (32%)
  Pallas kernels  2.87 us (12%)
  local copies, waits for them, and re-layouts  1.04 us (4%)
    ppermute x2, starting transfers between devices, passed_along(): return lax.ppermute(block, 'chan', route)  5.09 us
    ppermute x4, waiting for transfers between devices, swapped(): return lax.ppermute(block, axis, [(k, k ^ m) for k in devices])  4.94 us
    ppermute x4, starting transfers between devices, swapped(): return lax.ppermute(block, axis, [(k, k ^ m) for k in devices])  4.01 us
    ppermute x2, starting transfers between devices, passed_across(): return lax.ppermute(block, ('chan', 'tm'), route)  3.59 us
    pallas_call x6, Pallas kernels, call(): pl.pallas_call(kernel, out_shape=out_shape, in_specs=[spec] * len(inputs)...  2.87 us
    ppermute x2, waiting for transfers between devices, passed_across(): return lax.ppermute(block, ('chan', 'tm'), route)  1.64 us
    ppermute x2, waiting for transfers between devices, passed_along(): return lax.ppermute(block, 'chan', route)  1.44 us
    unnamed x2, local copies, waits for them, and re-layouts  1.04 us
  transfers between devices with their start and end apart: 8, of which 7 were waited for; matrix products, arithmetic and copies ran while one was open for 0% of the time, Pallas kernels for 2%

profile of v3, /device:TPU:0, one launch (start us, length us, event | category | flops | bytes accessed | tf_op | source)
XLA Modules:
  0.0 24.6 jit_solution(10363934256516140164)
XLA Ops:
  0.0 0.5 %collective-permute-start = (f32[256,512]{1,0:T(8,128)}, f32[256,512]{1,0:T(8,128)S(1)}, u32[]{:S(2)}, u32[]{:S(2)}) collective-permute-start(f32[256,512]{1,0:T(8,128)} %x_ref.1), channel_id=1, source_target_pairs={{0,1},{1,0},{2,3},{3,2},{4,5},{5,4},{6,7},{7,6},{8,9},{9,8},{10,11... | collective-permute-start | bytes 1572872 | tf_op jit(solution)/shard_map/ppermute | solution.py:288
  0.5 0.0 copy-start
  0.5 1.0 %copy-done = f32[256,512]{1,0:T(8,128)S(1)} copy-done((f32[256,512]{1,0:T(8,128)S(1)}, f32[256,512]{1,0:T(8,128)}, u32[]{:S(2)}) %copy-start) | copy-done | bytes 524312
  1.5 0.7 %collective-permute-done.other_ref = f32[256,512]{1,0:T(8,128)S(1)} collective-permute-done((f32[256,512]{1,0:T(8,128)}, f32[256,512]{1,0:T(8,128)S(1)}, u32[]{:S(2)}, u32[]{:S(2)}) %collective-permute-start) | collective-permute-done | bytes 524320 | tf_op jit(solution)/shard_map/ppermute | solution.py:288
  2.2 0.2 shard_map.19
  2.4 3.0 %collective-permute-start.2 = (bf16[8,1280]{1,0:T(8,128)(2,1)S(1)}, bf16[8,1280]{1,0:T(8,128)(2,1)S(1)}, u32[]{:S(2)}, u32[]{:S(2)}) collective-permute-start(bf16[8,1280]{1,0:T(8,128)(2,1)S(1)} %shard_map.19), channel_id=1, source_target_pairs={{24,0},{0,8},{8,16},{16,24},{25,1},{1,9},{9,17},{17,25},{26,2},{2,... | collective-permute-start | bytes 61448 | tf_op jit(solution)/shard_map/ppermute | solution.py:294
  5.4 2.1 %collective-permute-start.1 = (bf16[8,1280]{1,0:T(8,128)(2,1)S(1)}, bf16[8,1280]{1,0:T(8,128)(2,1)S(1)}, u32[]{:S(2)}, u32[]{:S(2)}) collective-permute-start(bf16[8,1280]{1,0:T(8,128)(2,1)S(1)} %shard_map.19), channel_id=1, source_target_pairs={{8,0},{16,8},{24,16},{0,24},{9,1},{17,9},{25,17},{1,25},{10,2},{18... | collective-permute-start | bytes 61448 | tf_op jit(solution)/shard_map/ppermute | solution.py:294
  7.5 0.5 %shard_map.18.receivers_ref = bf16[128,1152]{1,0:T(8,128)(2,1)S(1)} custom-call(f32[136,512]{1,0:T(8,128)S(1)} %shard_map.17.own_ref, f32[256,512]{1,0:T(8,128)S(1)} %collective-permute-done.other_ref), custom_call_target="tpu_custom_call" | custom-call | flops 536870912 | bytes 802816 | tf_op jit(solution)/shard_map/pallas_call | solution.py:273
  8.0 1.3 %collective-permute-done.2.refs_1_ = bf16[8,1280]{1,0:T(8,128)(2,1)S(1)} collective-permute-done((bf16[8,1280]{1,0:T(8,128)(2,1)S(1)}, bf16[8,1280]{1,0:T(8,128)(2,1)S(1)}, u32[]{:S(2)}, u32[]{:S(2)}) %collective-permute-start.2) | collective-permute-done | bytes 20512 | tf_op jit(solution)/shard_map/ppermute | solution.py:294
  9.3 0.1 collective-permute-done.1.refs_0_
  9.4 0.1 shard_map.20
  9.5 2.5 %collective-permute-start.3 = (bf16[448,128]{1,0:T(8,128)(2,1)S(1)}, bf16[448,128]{1,0:T(8,128)(2,1)S(1)}, u32[]{:S(2)}, u32[]{:S(2)}) collective-permute-start(bf16[448,128]{1,0:T(8,128)(2,1)S(1)} %get-tuple-element.12), channel_id=1, source_target_pairs={{0,6},{1,7},{2,4},{3,5},{4,2},{5,3},{6,0},{7,1},{8,14},{9,15},{10,... | collective-permute-start | bytes 344072 | tf_op jit(solution)/shard_map/ppermute | solution.py:288
  12.0 0.5 %collective-permute-start.4 = (bf16[448,128]{1,0:T(8,128)(2,1)S(1)}, bf16[448,128]{1,0:T(8,128)(2,1)S(1)}, u32[]{:S(2)}, u32[]{:S(2)}) collective-permute-start(bf16[448,128]{1,0:T(8,128)(2,1)S(1)} %get-tuple-element.13), channel_id=1, source_target_pairs={{0,4},{1,5},{2,6},{3,7},{4,0},{5,1},{6,2},{7,3},{8,12},{9,13},{10,... | collective-permute-start | bytes 344072 | tf_op jit(solution)/shard_map/ppermute | solution.py:288
  12.5 0.5 %collective-permute-start.5 = (bf16[448,128]{1,0:T(8,128)(2,1)S(1)}, bf16[448,128]{1,0:T(8,128)(2,1)S(1)}, u32[]{:S(2)}, u32[]{:S(2)}) collective-permute-start(bf16[448,128]{1,0:T(8,128)(2,1)S(1)} %get-tuple-element.14), channel_id=1, source_target_pairs={{0,2},{1,3},{2,0},{3,1},{4,6},{5,7},{6,4},{7,5},{8,10},{9,11},{10,... | collective-permute-start | bytes 344072 | tf_op jit(solution)/shard_map/ppermute | solution.py:288
  13.0 3.0 %collective-permute-done.3.refs_1_ = bf16[448,128]{1,0:T(8,128)(2,1)S(1)} collective-permute-done((bf16[448,128]{1,0:T(8,128)(2,1)S(1)}, bf16[448,128]{1,0:T(8,128)(2,1)S(1)}, u32[]{:S(2)}, u32[]{:S(2)}) %collective-permute-start.3) | collective-permute-done | bytes 114720 | tf_op jit(solution)/shard_map/ppermute | solution.py:288
  16.0 1.1 %collective-permute-done.4.refs_2_ = bf16[448,128]{1,0:T(8,128)(2,1)S(1)} collective-permute-done((bf16[448,128]{1,0:T(8,128)(2,1)S(1)}, bf16[448,128]{1,0:T(8,128)(2,1)S(1)}, u32[]{:S(2)}, u32[]{:S(2)}) %collective-permute-start.4) | collective-permute-done | bytes 114720 | tf_op jit(solution)/shard_map/ppermute | solution.py:288
  17.1 0.2 %collective-permute-done.5.refs_3_ = bf16[448,128]{1,0:T(8,128)(2,1)S(1)} collective-permute-done((bf16[448,128]{1,0:T(8,128)(2,1)S(1)}, bf16[448,128]{1,0:T(8,128)(2,1)S(1)}, u32[]{:S(2)}, u32[]{:S(2)}) %collective-permute-start.5) | collective-permute-done | bytes 114720 | tf_op jit(solution)/shard_map/ppermute | solution.py:288
  17.3 1.4 %shard_map.21 = (bf16[8,1632]{1,0:T(8,128)(2,1)S(1)}, bf16[8,1632]{1,0:T(8,128)(2,1)S(1)}) custom-call(bf16[448,128]{1,0:T(8,128)(2,1)S(1)} %get-tuple-element.11.refs_0_, bf16[448,128]{1,0:T(8,128)(2,1)S(1)} %collective-permute-done.3.refs_1_, bf16[448,128]{1,0:T(8,128)(2,1)S(1)} %collective-permute-done.4.refs_2_, ...), custom_call_target="tpu_custom_call" | custom-call | flops 293601280 | bytes 458752 | tf_op jit(solution)/shard_map/pallas_call | solution.py:273
  18.7 0.1 collective-permute-start.6
  18.8 3.5 %collective-permute-start.7 = (bf16[8,1632]{1,0:T(8,128)(2,1)S(1)}, bf16[8,1632]{1,0:T(8,128)(2,1)S(1)}, u32[]{:S(2)}, u32[]{:S(2)}) collective-permute-start(bf16[8,1632]{1,0:T(8,128)(2,1)S(1)} %get-tuple-element.16), channel_id=1, source_target_pairs={{9,0},{8,1},{11,2},{10,3},{13,4},{12,5},{15,6},{14,7},{17,8},{16,9... | collective-permute-start | bytes 78344 | tf_op jit(solution)/shard_map/ppermute | solution.py:304
  22.3 1.6 %collective-permute-done.6.refs_0_ = bf16[8,1632]{1,0:T(8,128)(2,1)S(1)} collective-permute-done((bf16[8,1632]{1,0:T(8,128)(2,1)S(1)}, bf16[8,1632]{1,0:T(8,128)(2,1)S(1)}, u32[]{:S(2)}, u32[]{:S(2)}) %collective-permute-start.6) | collective-permute-done | bytes 26144 | tf_op jit(solution)/shard_map/ppermute | solution.py:304
  24.0 0.0 collective-permute-done.7.refs_1_
  24.0 0.7 %shard_map.22 = f32[8,2,1632]{2,1,0:T(2,128)} custom-call(bf16[8,1632]{1,0:T(8,128)(2,1)S(1)} %collective-permute-done.6.refs_0_, bf16[8,1632]{1,0:T(8,128)(2,1)S(1)} %collective-permute-done.7.refs_1_), custom_call_target="tpu_custom_call" | custom-call | bytes 52224 | tf_op jit(solution)/shard_map/pallas_call | solution.py:273
  (1 shorter events, 0.0 us)
Async XLA Ops:
  0.0 2.2 %collective-permute-start = (f32[256,512]{1,0:T(8,128)}, f32[256,512]{1,0:T(8,128)S(1)}, u32[]{:S(2)}, u32[]{:S(2)}) collective-permute-start(f32[256,512]{1,0:T(8,128)} %x_ref.1), channel_id=1, source_target_pairs={{0,1},{1,0},{2,3},{3,2},{4,5},{5,4},{6,7},{7,6},{8,9},{9,8},{10,11... | collective-permute-start | bytes 1572872 | tf_op jit(solution)/shard_map/ppermute | solution.py:288
  0.5 1.0 %copy-start = (f32[256,512]{1,0:T(8,128)S(1)}, f32[256,512]{1,0:T(8,128)}, u32[]{:S(2)}) copy-start(f32[256,512]{1,0:T(8,128)} %x_ref.1) | copy-start | bytes 1572868
  2.4 6.9 %collective-permute-start.2 = (bf16[8,1280]{1,0:T(8,128)(2,1)S(1)}, bf16[8,1280]{1,0:T(8,128)(2,1)S(1)}, u32[]{:S(2)}, u32[]{:S(2)}) collective-permute-start(bf16[8,1280]{1,0:T(8,128)(2,1)S(1)} %shard_map.19), channel_id=1, source_target_pairs={{24,0},{0,8},{8,16},{16,24},{25,1},{1,9},{9,17},{17,25},{26,2},{2,... | collective-permute-start | bytes 61448 | tf_op jit(solution)/shard_map/ppermute | solution.py:294
  5.4 4.0 %collective-permute-start.1 = (bf16[8,1280]{1,0:T(8,128)(2,1)S(1)}, bf16[8,1280]{1,0:T(8,128)(2,1)S(1)}, u32[]{:S(2)}, u32[]{:S(2)}) collective-permute-start(bf16[8,1280]{1,0:T(8,128)(2,1)S(1)} %shard_map.19), channel_id=1, source_target_pairs={{8,0},{16,8},{24,16},{0,24},{9,1},{17,9},{25,17},{1,25},{10,2},{18... | collective-permute-start | bytes 61448 | tf_op jit(solution)/shard_map/ppermute | solution.py:294
  9.5 6.5 %collective-permute-start.3 = (bf16[448,128]{1,0:T(8,128)(2,1)S(1)}, bf16[448,128]{1,0:T(8,128)(2,1)S(1)}, u32[]{:S(2)}, u32[]{:S(2)}) collective-permute-start(bf16[448,128]{1,0:T(8,128)(2,1)S(1)} %get-tuple-element.12), channel_id=1, source_target_pairs={{0,6},{1,7},{2,4},{3,5},{4,2},{5,3},{6,0},{7,1},{8,14},{9,15},{10,... | collective-permute-start | bytes 344072 | tf_op jit(solution)/shard_map/ppermute | solution.py:288
  12.0 5.0 %collective-permute-start.4 = (bf16[448,128]{1,0:T(8,128)(2,1)S(1)}, bf16[448,128]{1,0:T(8,128)(2,1)S(1)}, u32[]{:S(2)}, u32[]{:S(2)}) collective-permute-start(bf16[448,128]{1,0:T(8,128)(2,1)S(1)} %get-tuple-element.13), channel_id=1, source_target_pairs={{0,4},{1,5},{2,6},{3,7},{4,0},{5,1},{6,2},{7,3},{8,12},{9,13},{10,... | collective-permute-start | bytes 344072 | tf_op jit(solution)/shard_map/ppermute | solution.py:288
  12.5 4.8 %collective-permute-start.5 = (bf16[448,128]{1,0:T(8,128)(2,1)S(1)}, bf16[448,128]{1,0:T(8,128)(2,1)S(1)}, u32[]{:S(2)}, u32[]{:S(2)}) collective-permute-start(bf16[448,128]{1,0:T(8,128)(2,1)S(1)} %get-tuple-element.14), channel_id=1, source_target_pairs={{0,2},{1,3},{2,0},{3,1},{4,6},{5,7},{6,4},{7,5},{8,10},{9,11},{10,... | collective-permute-start | bytes 344072 | tf_op jit(solution)/shard_map/ppermute | solution.py:288
  18.7 5.2 %collective-permute-start.6 = (bf16[8,1632]{1,0:T(8,128)(2,1)S(1)}, bf16[8,1632]{1,0:T(8,128)(2,1)S(1)}, u32[]{:S(2)}, u32[]{:S(2)}) collective-permute-start(bf16[8,1632]{1,0:T(8,128)(2,1)S(1)} %get-tuple-element.15), channel_id=1, source_target_pairs={{25,0},{24,1},{27,2},{26,3},{29,4},{28,5},{31,6},{30,7},{1,8},{0,9... | collective-permute-start | bytes 78344 | tf_op jit(solution)/shard_map/ppermute | solution.py:304
  18.8 5.2 %collective-permute-start.7 = (bf16[8,1632]{1,0:T(8,128)(2,1)S(1)}, bf16[8,1632]{1,0:T(8,128)(2,1)S(1)}, u32[]{:S(2)}, u32[]{:S(2)}) collective-permute-start(bf16[8,1632]{1,0:T(8,128)(2,1)S(1)} %get-tuple-element.16), channel_id=1, source_target_pairs={{9,0},{8,1},{11,2},{10,3},{13,4},{12,5},{15,6},{14,7},{17,8},{16,9... | collective-permute-start | bytes 78344 | tf_op jit(solution)/shard_map/ppermute | solution.py:304

commit v4 on v2

--- a/solution.py
+++ b/solution.py
@@ -196,7 +196,7 @@
     outs, (held, mixed, table) = refs[:offsets], refs[offsets:]
     sources = offsets * SRC
     group = held.shape[1] - sources
-    runs = [ref[...].astype(held.dtype) for ref in blocks[:1] + blocks[:0:-1]]
+    runs = {m: ref[...].astype(held.dtype) for m, ref in zip(chip_order(chips), blocks)}
     product = None
     for wide in finished_shards(runs, held):
         receivers, senders = wide[:group], wide[group:]
@@ -275,6 +275,10 @@
     )(*inputs)
 
 
+def chip_order(chips):
+    return [m for m in (0, 2, 3, 1) if m < chips] + list(range(4, chips))
+
+
 def swapped(block, axis, m):
     devices = range(lax.axis_size(axis))
     return lax.ppermute(block, axis, [(k, k ^ m) for k in devices])
@@ -334,7 +338,7 @@
         [own_receivers] + arrived,
     )
     blocks = list(blocks[:1]) + [
-        swapped(blocks[m], "tm", CORES * m) for m in range(chips - 1, 0, -1)
+        swapped(blocks[m], "tm", CORES * m) for m in chip_order(chips)[1:]
     ]
     columns = -(-group * FINE // LANES) * LANES
     heights = -(-COARSE * sources // LANES) * LANES

time: 24.9 us -> 25.1 us (level)
  no operation moved by 1% of the time
where the time goes in v4:
time: 25.1 us; the launch traced here: 24.9 us
  starting transfers between devices  12.7 us (51%)
  waiting for transfers between devices  8.3 us (33%)
  Pallas kernels  2.84 us (11%)
  local copies, waits for them, and re-layouts  1.04 us (4%)
    ppermute x4, waiting for transfers between devices, swapped(): return lax.ppermute(block, axis, [(k, k ^ m) for k in devices])  5.33 us
    ppermute x2, starting transfers between devices, passed_along(): return lax.ppermute(block, 'chan', route)  5.09 us
    ppermute x4, starting transfers between devices, swapped(): return lax.ppermute(block, axis, [(k, k ^ m) for k in devices])  4.01 us
    ppermute x2, starting transfers between devices, passed_across(): return lax.ppermute(block, ('chan', 'tm'), route)  3.59 us
    pallas_call x6, Pallas kernels, call(): pl.pallas_call(kernel, out_shape=out_shape, in_specs=[spec] * len(inputs)...  2.84 us
    ppermute x2, waiting for transfers between devices, passed_across(): return lax.ppermute(block, ('chan', 'tm'), route)  1.54 us
    ppermute x2, waiting for transfers between devices, passed_along(): return lax.ppermute(block, 'chan', route)  1.43 us
    unnamed x2, local copies, waits for them, and re-layouts  1.04 us
  transfers between devices with their start and end apart: 8, of which 7 were waited for; matrix products, arithmetic and copies ran while one was open for 0% of the time, Pallas kernels for 2%

profile of v4, /device:TPU:0, one launch (start us, length us, event | category | flops | bytes accessed | tf_op | source)
XLA Modules:
  0.0 24.9 jit_solution(7148371781278596235)
XLA Ops:
  0.0 0.5 %collective-permute-start = (f32[256,512]{1,0:T(8,128)}, f32[256,512]{1,0:T(8,128)S(1)}, u32[]{:S(2)}, u32[]{:S(2)}) collective-permute-start(f32[256,512]{1,0:T(8,128)} %x_ref.1), channel_id=1, source_target_pairs={{0,1},{1,0},{2,3},{3,2},{4,5},{5,4},{6,7},{7,6},{8,9},{9,8},{10,11... | collective-permute-start | bytes 1572872 | tf_op jit(solution)/shard_map/ppermute | solution.py:284
  0.5 0.0 copy-start
  0.5 1.0 %copy-done = f32[256,512]{1,0:T(8,128)S(1)} copy-done((f32[256,512]{1,0:T(8,128)S(1)}, f32[256,512]{1,0:T(8,128)}, u32[]{:S(2)}) %copy-start) | copy-done | bytes 524312
  1.5 0.7 %collective-permute-done.other_ref = f32[256,512]{1,0:T(8,128)S(1)} collective-permute-done((f32[256,512]{1,0:T(8,128)}, f32[256,512]{1,0:T(8,128)S(1)}, u32[]{:S(2)}, u32[]{:S(2)}) %collective-permute-start) | collective-permute-done | bytes 524320 | tf_op jit(solution)/shard_map/ppermute | solution.py:284
  2.2 0.2 shard_map.19
  2.4 3.0 %collective-permute-start.2 = (bf16[8,1280]{1,0:T(8,128)(2,1)S(1)}, bf16[8,1280]{1,0:T(8,128)(2,1)S(1)}, u32[]{:S(2)}, u32[]{:S(2)}) collective-permute-start(bf16[8,1280]{1,0:T(8,128)(2,1)S(1)} %shard_map.19), channel_id=1, source_target_pairs={{24,0},{0,8},{8,16},{16,24},{25,1},{1,9},{9,17},{17,25},{26,2},{2,... | collective-permute-start | bytes 61448 | tf_op jit(solution)/shard_map/ppermute | solution.py:290
  5.4 2.1 %collective-permute-start.1 = (bf16[8,1280]{1,0:T(8,128)(2,1)S(1)}, bf16[8,1280]{1,0:T(8,128)(2,1)S(1)}, u32[]{:S(2)}, u32[]{:S(2)}) collective-permute-start(bf16[8,1280]{1,0:T(8,128)(2,1)S(1)} %shard_map.19), channel_id=1, source_target_pairs={{8,0},{16,8},{24,16},{0,24},{9,1},{17,9},{25,17},{1,25},{10,2},{18... | collective-permute-start | bytes 61448 | tf_op jit(solution)/shard_map/ppermute | solution.py:290
  7.5 0.5 %shard_map.18.receivers_ref = bf16[128,1280]{1,0:T(8,128)(2,1)S(1)} custom-call(f32[136,512]{1,0:T(8,128)S(1)} %shard_map.17.own_ref, f32[256,512]{1,0:T(8,128)S(1)} %collective-permute-done.other_ref), custom_call_target="tpu_custom_call" | custom-call | flops 536870912 | bytes 802816 | tf_op jit(solution)/shard_map/pallas_call | solution.py:265
  8.0 1.3 %collective-permute-done.2.refs_1_ = bf16[8,1280]{1,0:T(8,128)(2,1)S(1)} collective-permute-done((bf16[8,1280]{1,0:T(8,128)(2,1)S(1)}, bf16[8,1280]{1,0:T(8,128)(2,1)S(1)}, u32[]{:S(2)}, u32[]{:S(2)}) %collective-permute-start.2) | collective-permute-done | bytes 20512 | tf_op jit(solution)/shard_map/ppermute | solution.py:290
  9.3 0.1 collective-permute-done.1.refs_0_
  9.5 1.6 %collective-permute-start.3 = (bf16[48,1280]{1,0:T(8,128)(2,1)S(1)}, bf16[48,1280]{1,0:T(8,128)(2,1)S(1)}, u32[]{:S(2)}, u32[]{:S(2)}) collective-permute-start(bf16[48,1280]{1,0:T(8,128)(2,1)S(1)} %get-tuple-element.12), channel_id=1, source_target_pairs={{0,4},{1,5},{2,6},{3,7},{4,0},{5,1},{6,2},{7,3},{8,12},{9,13},{10,... | collective-permute-start | bytes 368648 | tf_op jit(solution)/shard_map/ppermute | solution.py:284
  11.1 1.4 %collective-permute-start.4 = (bf16[48,1280]{1,0:T(8,128)(2,1)S(1)}, bf16[48,1280]{1,0:T(8,128)(2,1)S(1)}, u32[]{:S(2)}, u32[]{:S(2)}) collective-permute-start(bf16[48,1280]{1,0:T(8,128)(2,1)S(1)} %get-tuple-element.13), channel_id=1, source_target_pairs={{0,6},{1,7},{2,4},{3,5},{4,2},{5,3},{6,0},{7,1},{8,14},{9,15},{10,... | collective-permute-start | bytes 368648 | tf_op jit(solution)/shard_map/ppermute | solution.py:284
  12.5 0.5 %collective-permute-start.5 = (bf16[48,1280]{1,0:T(8,128)(2,1)S(1)}, bf16[48,1280]{1,0:T(8,128)(2,1)S(1)}, u32[]{:S(2)}, u32[]{:S(2)}) collective-permute-start(bf16[48,1280]{1,0:T(8,128)(2,1)S(1)} %get-tuple-element.14), channel_id=1, source_target_pairs={{0,2},{1,3},{2,0},{3,1},{4,6},{5,7},{6,4},{7,5},{8,10},{9,11},{10,... | collective-permute-start | bytes 368648 | tf_op jit(solution)/shard_map/ppermute | solution.py:284
  13.0 2.8 %collective-permute-done.3.refs_1_ = bf16[48,1280]{1,0:T(8,128)(2,1)S(1)} collective-permute-done((bf16[48,1280]{1,0:T(8,128)(2,1)S(1)}, bf16[48,1280]{1,0:T(8,128)(2,1)S(1)}, u32[]{:S(2)}, u32[]{:S(2)}) %collective-permute-start.3) | collective-permute-done | bytes 122912 | tf_op jit(solution)/shard_map/ppermute | solution.py:284
  15.9 1.5 %collective-permute-done.4.refs_2_ = bf16[48,1280]{1,0:T(8,128)(2,1)S(1)} collective-permute-done((bf16[48,1280]{1,0:T(8,128)(2,1)S(1)}, bf16[48,1280]{1,0:T(8,128)(2,1)S(1)}, u32[]{:S(2)}, u32[]{:S(2)}) %collective-permute-start.4) | collective-permute-done | bytes 122912 | tf_op jit(solution)/shard_map/ppermute | solution.py:284
  17.3 0.4 %collective-permute-done.5.refs_3_ = bf16[48,1280]{1,0:T(8,128)(2,1)S(1)} collective-permute-done((bf16[48,1280]{1,0:T(8,128)(2,1)S(1)}, bf16[48,1280]{1,0:T(8,128)(2,1)S(1)}, u32[]{:S(2)}, u32[]{:S(2)}) %collective-permute-start.5) | collective-permute-done | bytes 122912 | tf_op jit(solution)/shard_map/ppermute | solution.py:284
  17.7 1.4 %shard_map.21 = (bf16[8,1632]{1,0:T(8,128)(2,1)S(1)}, bf16[8,1632]{1,0:T(8,128)(2,1)S(1)}) custom-call(bf16[48,1280]{1,0:T(8,128)(2,1)S(1)} %get-tuple-element.11.refs_0_, bf16[48,1280]{1,0:T(8,128)(2,1)S(1)} %collective-permute-done.3.refs_1_, bf16[48,1280]{1,0:T(8,128)(2,1)S(1)} %collective-permute-done.4.refs_2_, ...), custom_call_target="tpu_custom_call" | custom-call | flops 293601280 | bytes 491520 | tf_op jit(solution)/shard_map/pallas_call | solution.py:265
  19.1 0.1 collective-permute-start.6
  19.2 3.5 %collective-permute-start.7 = (bf16[8,1632]{1,0:T(8,128)(2,1)S(1)}, bf16[8,1632]{1,0:T(8,128)(2,1)S(1)}, u32[]{:S(2)}, u32[]{:S(2)}) collective-permute-start(bf16[8,1632]{1,0:T(8,128)(2,1)S(1)} %get-tuple-element.16), channel_id=1, source_target_pairs={{9,0},{8,1},{11,2},{10,3},{13,4},{12,5},{15,6},{14,7},{17,8},{16,9... | collective-permute-start | bytes 78344 | tf_op jit(solution)/shard_map/ppermute | solution.py:300
  22.7 1.5 %collective-permute-done.6.refs_0_ = bf16[8,1632]{1,0:T(8,128)(2,1)S(1)} collective-permute-done((bf16[8,1632]{1,0:T(8,128)(2,1)S(1)}, bf16[8,1632]{1,0:T(8,128)(2,1)S(1)}, u32[]{:S(2)}, u32[]{:S(2)}) %collective-permute-start.6) | collective-permute-done | bytes 26144 | tf_op jit(solution)/shard_map/ppermute | solution.py:300
  24.2 0.0 collective-permute-done.7.refs_1_
  24.2 0.7 %shard_map.22 = f32[8,2,1632]{2,1,0:T(2,128)} custom-call(bf16[8,1632]{1,0:T(8,128)(2,1)S(1)} %collective-permute-done.6.refs_0_, bf16[8,1632]{1,0:T(8,128)(2,1)S(1)} %collective-permute-done.7.refs_1_), custom_call_target="tpu_custom_call" | custom-call | bytes 52224 | tf_op jit(solution)/shard_map/pallas_call | solution.py:265
  (2 shorter events, 0.1 us)
Async XLA Ops:
  0.0 2.2 %collective-permute-start = (f32[256,512]{1,0:T(8,128)}, f32[256,512]{1,0:T(8,128)S(1)}, u32[]{:S(2)}, u32[]{:S(2)}) collective-permute-start(f32[256,512]{1,0:T(8,128)} %x_ref.1), channel_id=1, source_target_pairs={{0,1},{1,0},{2,3},{3,2},{4,5},{5,4},{6,7},{7,6},{8,9},{9,8},{10,11... | collective-permute-start | bytes 1572872 | tf_op jit(solution)/shard_map/ppermute | solution.py:284
  0.5 1.0 %copy-start = (f32[256,512]{1,0:T(8,128)S(1)}, f32[256,512]{1,0:T(8,128)}, u32[]{:S(2)}) copy-start(f32[256,512]{1,0:T(8,128)} %x_ref.1) | copy-start | bytes 1572868
  2.4 6.9 %collective-permute-start.2 = (bf16[8,1280]{1,0:T(8,128)(2,1)S(1)}, bf16[8,1280]{1,0:T(8,128)(2,1)S(1)}, u32[]{:S(2)}, u32[]{:S(2)}) collective-permute-start(bf16[8,1280]{1,0:T(8,128)(2,1)S(1)} %shard_map.19), channel_id=1, source_target_pairs={{24,0},{0,8},{8,16},{16,24},{25,1},{1,9},{9,17},{17,25},{26,2},{2,... | collective-permute-start | bytes 61448 | tf_op jit(solution)/shard_map/ppermute | solution.py:290
  5.4 4.0 %collective-permute-start.1 = (bf16[8,1280]{1,0:T(8,128)(2,1)S(1)}, bf16[8,1280]{1,0:T(8,128)(2,1)S(1)}, u32[]{:S(2)}, u32[]{:S(2)}) collective-permute-start(bf16[8,1280]{1,0:T(8,128)(2,1)S(1)} %shard_map.19), channel_id=1, source_target_pairs={{8,0},{16,8},{24,16},{0,24},{9,1},{17,9},{25,17},{1,25},{10,2},{18... | collective-permute-start | bytes 61448 | tf_op jit(solution)/shard_map/ppermute | solution.py:290
  9.5 6.4 %collective-permute-start.3 = (bf16[48,1280]{1,0:T(8,128)(2,1)S(1)}, bf16[48,1280]{1,0:T(8,128)(2,1)S(1)}, u32[]{:S(2)}, u32[]{:S(2)}) collective-permute-start(bf16[48,1280]{1,0:T(8,128)(2,1)S(1)} %get-tuple-element.12), channel_id=1, source_target_pairs={{0,4},{1,5},{2,6},{3,7},{4,0},{5,1},{6,2},{7,3},{8,12},{9,13},{10,... | collective-permute-start | bytes 368648 | tf_op jit(solution)/shard_map/ppermute | solution.py:284
  11.1 6.3 %collective-permute-start.4 = (bf16[48,1280]{1,0:T(8,128)(2,1)S(1)}, bf16[48,1280]{1,0:T(8,128)(2,1)S(1)}, u32[]{:S(2)}, u32[]{:S(2)}) collective-permute-start(bf16[48,1280]{1,0:T(8,128)(2,1)S(1)} %get-tuple-element.13), channel_id=1, source_target_pairs={{0,6},{1,7},{2,4},{3,5},{4,2},{5,3},{6,0},{7,1},{8,14},{9,15},{10,... | collective-permute-start | bytes 368648 | tf_op jit(solution)/shard_map/ppermute | solution.py:284
  12.5 5.2 %collective-permute-start.5 = (bf16[48,1280]{1,0:T(8,128)(2,1)S(1)}, bf16[48,1280]{1,0:T(8,128)(2,1)S(1)}, u32[]{:S(2)}, u32[]{:S(2)}) collective-permute-start(bf16[48,1280]{1,0:T(8,128)(2,1)S(1)} %get-tuple-element.14), channel_id=1, source_target_pairs={{0,2},{1,3},{2,0},{3,1},{4,6},{5,7},{6,4},{7,5},{8,10},{9,11},{10,... | collective-permute-start | bytes 368648 | tf_op jit(solution)/shard_map/ppermute | solution.py:284
  19.1 5.1 %collective-permute-start.6 = (bf16[8,1632]{1,0:T(8,128)(2,1)S(1)}, bf16[8,1632]{1,0:T(8,128)(2,1)S(1)}, u32[]{:S(2)}, u32[]{:S(2)}) collective-permute-start(bf16[8,1632]{1,0:T(8,128)(2,1)S(1)} %get-tuple-element.15), channel_id=1, source_target_pairs={{25,0},{24,1},{27,2},{26,3},{29,4},{28,5},{31,6},{30,7},{1,8},{0,9... | collective-permute-start | bytes 78344 | tf_op jit(solution)/shard_map/ppermute | solution.py:300
  19.2 5.1 %collective-permute-start.7 = (bf16[8,1632]{1,0:T(8,128)(2,1)S(1)}, bf16[8,1632]{1,0:T(8,128)(2,1)S(1)}, u32[]{:S(2)}, u32[]{:S(2)}) collective-permute-start(bf16[8,1632]{1,0:T(8,128)(2,1)S(1)} %get-tuple-element.16), channel_id=1, source_target_pairs={{9,0},{8,1},{11,2},{10,3},{13,4},{12,5},{15,6},{14,7},{17,8},{16,9... | collective-permute-start | bytes 78344 | tf_op jit(solution)/shard_map/ppermute | solution.py:300

commit v5 on v4

--- a/solution.py
+++ b/solution.py
@@ -276,7 +276,7 @@
 
 
 def chip_order(chips):
-    return [m for m in (0, 2, 3, 1) if m < chips] + list(range(4, chips))
+    return [m for m in (0, 3, 1, 2) if m < chips] + list(range(4, chips))
 
 
 def swapped(block, axis, m):

time: 25.1 us -> 24.9 us (level)
  no operation moved by 1% of the time
where the time goes in v5:
time: 24.9 us; the launch traced here: 24.8 us
  starting transfers between devices  12.7 us (51%)
  waiting for transfers between devices  8.18 us (33%)
  Pallas kernels  2.84 us (11%)
  local copies, waits for them, and re-layouts  1.04 us (4%)
    ppermute x4, waiting for transfers between devices, swapped(): return lax.ppermute(block, axis, [(k, k ^ m) for k in devices])  5.21 us
    ppermute x2, starting transfers between devices, passed_along(): return lax.ppermute(block, 'chan', route)  5.09 us
    ppermute x4, starting transfers between devices, swapped(): return lax.ppermute(block, axis, [(k, k ^ m) for k in devices])  4.01 us
    ppermute x2, starting transfers between devices, passed_across(): return lax.ppermute(block, ('chan', 'tm'), route)  3.59 us
    pallas_call x6, Pallas kernels, call(): pl.pallas_call(kernel, out_shape=out_shape, in_specs=[spec] * len(inputs)...  2.84 us
    ppermute x2, waiting for transfers between devices, passed_across(): return lax.ppermute(block, ('chan', 'tm'), route)  1.54 us
    ppermute x2, waiting for transfers between devices, passed_along(): return lax.ppermute(block, 'chan', route)  1.43 us
    unnamed x2, local copies, waits for them, and re-layouts  1.04 us
  transfers between devices with their start and end apart: 8, of which 7 were waited for; matrix products, arithmetic and copies ran while one was open for 0% of the time, Pallas kernels for 2%

profile of v5, /device:TPU:0, one launch (start us, length us, event | category | flops | bytes accessed | tf_op | source)
XLA Modules:
  0.0 24.8 jit_solution(6083557831626369209)
XLA Ops:
  0.0 0.5 %collective-permute-start = (f32[256,512]{1,0:T(8,128)}, f32[256,512]{1,0:T(8,128)S(1)}, u32[]{:S(2)}, u32[]{:S(2)}) collective-permute-start(f32[256,512]{1,0:T(8,128)} %x_ref.1), channel_id=1, source_target_pairs={{0,1},{1,0},{2,3},{3,2},{4,5},{5,4},{6,7},{7,6},{8,9},{9,8},{10,11... | collective-permute-start | bytes 1572872 | tf_op jit(solution)/shard_map/ppermute | solution.py:284
  0.5 0.0 copy-start
  0.5 1.0 %copy-done = f32[256,512]{1,0:T(8,128)S(1)} copy-done((f32[256,512]{1,0:T(8,128)S(1)}, f32[256,512]{1,0:T(8,128)}, u32[]{:S(2)}) %copy-start) | copy-done | bytes 524312
  1.5 0.7 %collective-permute-done.other_ref = f32[256,512]{1,0:T(8,128)S(1)} collective-permute-done((f32[256,512]{1,0:T(8,128)}, f32[256,512]{1,0:T(8,128)S(1)}, u32[]{:S(2)}, u32[]{:S(2)}) %collective-permute-start) | collective-permute-done | bytes 524320 | tf_op jit(solution)/shard_map/ppermute | solution.py:284
  2.2 0.2 shard_map.19
  2.4 3.0 %collective-permute-start.2 = (bf16[8,1280]{1,0:T(8,128)(2,1)S(1)}, bf16[8,1280]{1,0:T(8,128)(2,1)S(1)}, u32[]{:S(2)}, u32[]{:S(2)}) collective-permute-start(bf16[8,1280]{1,0:T(8,128)(2,1)S(1)} %shard_map.19), channel_id=1, source_target_pairs={{24,0},{0,8},{8,16},{16,24},{25,1},{1,9},{9,17},{17,25},{26,2},{2,... | collective-permute-start | bytes 61448 | tf_op jit(solution)/shard_map/ppermute | solution.py:290
  5.4 2.1 %collective-permute-start.1 = (bf16[8,1280]{1,0:T(8,128)(2,1)S(1)}, bf16[8,1280]{1,0:T(8,128)(2,1)S(1)}, u32[]{:S(2)}, u32[]{:S(2)}) collective-permute-start(bf16[8,1280]{1,0:T(8,128)(2,1)S(1)} %shard_map.19), channel_id=1, source_target_pairs={{8,0},{16,8},{24,16},{0,24},{9,1},{17,9},{25,17},{1,25},{10,2},{18... | collective-permute-start | bytes 61448 | tf_op jit(solution)/shard_map/ppermute | solution.py:290
  7.5 0.5 %shard_map.18.receivers_ref = bf16[128,1280]{1,0:T(8,128)(2,1)S(1)} custom-call(f32[136,512]{1,0:T(8,128)S(1)} %shard_map.17.own_ref, f32[256,512]{1,0:T(8,128)S(1)} %collective-permute-done.other_ref), custom_call_target="tpu_custom_call" | custom-call | flops 536870912 | bytes 802816 | tf_op jit(solution)/shard_map/pallas_call | solution.py:265
  8.0 1.3 %collective-permute-done.2.refs_1_ = bf16[8,1280]{1,0:T(8,128)(2,1)S(1)} collective-permute-done((bf16[8,1280]{1,0:T(8,128)(2,1)S(1)}, bf16[8,1280]{1,0:T(8,128)(2,1)S(1)}, u32[]{:S(2)}, u32[]{:S(2)}) %collective-permute-start.2) | collective-permute-done | bytes 20512 | tf_op jit(solution)/shard_map/ppermute | solution.py:290
  9.3 0.1 collective-permute-done.1.refs_0_
  9.5 2.5 %collective-permute-start.3 = (bf16[48,1280]{1,0:T(8,128)(2,1)S(1)}, bf16[48,1280]{1,0:T(8,128)(2,1)S(1)}, u32[]{:S(2)}, u32[]{:S(2)}) collective-permute-start(bf16[48,1280]{1,0:T(8,128)(2,1)S(1)} %get-tuple-element.12), channel_id=1, source_target_pairs={{0,6},{1,7},{2,4},{3,5},{4,2},{5,3},{6,0},{7,1},{8,14},{9,15},{10,... | collective-permute-start | bytes 368648 | tf_op jit(solution)/shard_map/ppermute | solution.py:284
  12.0 0.5 %collective-permute-start.4 = (bf16[48,1280]{1,0:T(8,128)(2,1)S(1)}, bf16[48,1280]{1,0:T(8,128)(2,1)S(1)}, u32[]{:S(2)}, u32[]{:S(2)}) collective-permute-start(bf16[48,1280]{1,0:T(8,128)(2,1)S(1)} %get-tuple-element.13), channel_id=1, source_target_pairs={{0,2},{1,3},{2,0},{3,1},{4,6},{5,7},{6,4},{7,5},{8,10},{9,11},{10,... | collective-permute-start | bytes 368648 | tf_op jit(solution)/shard_map/ppermute | solution.py:284
  12.5 0.5 %collective-permute-start.5 = (bf16[48,1280]{1,0:T(8,128)(2,1)S(1)}, bf16[48,1280]{1,0:T(8,128)(2,1)S(1)}, u32[]{:S(2)}, u32[]{:S(2)}) collective-permute-start(bf16[48,1280]{1,0:T(8,128)(2,1)S(1)} %get-tuple-element.14), channel_id=1, source_target_pairs={{0,4},{1,5},{2,6},{3,7},{4,0},{5,1},{6,2},{7,3},{8,12},{9,13},{10,... | collective-permute-start | bytes 368648 | tf_op jit(solution)/shard_map/ppermute | solution.py:284
  13.0 3.1 %collective-permute-done.3.refs_1_ = bf16[48,1280]{1,0:T(8,128)(2,1)S(1)} collective-permute-done((bf16[48,1280]{1,0:T(8,128)(2,1)S(1)}, bf16[48,1280]{1,0:T(8,128)(2,1)S(1)}, u32[]{:S(2)}, u32[]{:S(2)}) %collective-permute-start.3) | collective-permute-done | bytes 122912 | tf_op jit(solution)/shard_map/ppermute | solution.py:284
  16.1 1.3 %collective-permute-done.4.refs_2_ = bf16[48,1280]{1,0:T(8,128)(2,1)S(1)} collective-permute-done((bf16[48,1280]{1,0:T(8,128)(2,1)S(1)}, bf16[48,1280]{1,0:T(8,128)(2,1)S(1)}, u32[]{:S(2)}, u32[]{:S(2)}) %collective-permute-start.4) | collective-permute-done | bytes 122912 | tf_op jit(solution)/shard_map/ppermute | solution.py:284
  17.4 0.1 collective-permute-done.5.refs_3_
  17.5 1.4 %shard_map.21 = (bf16[8,1632]{1,0:T(8,128)(2,1)S(1)}, bf16[8,1632]{1,0:T(8,128)(2,1)S(1)}) custom-call(bf16[48,1280]{1,0:T(8,128)(2,1)S(1)} %get-tuple-element.11.refs_0_, bf16[48,1280]{1,0:T(8,128)(2,1)S(1)} %collective-permute-done.3.refs_1_, bf16[48,1280]{1,0:T(8,128)(2,1)S(1)} %collective-permute-done.4.refs_2_, ...), custom_call_target="tpu_custom_call" | custom-call | flops 293601280 | bytes 491520 | tf_op jit(solution)/shard_map/pallas_call | solution.py:265
  19.0 0.1 collective-permute-start.6
  19.0 3.5 %collective-permute-start.7 = (bf16[8,1632]{1,0:T(8,128)(2,1)S(1)}, bf16[8,1632]{1,0:T(8,128)(2,1)S(1)}, u32[]{:S(2)}, u32[]{:S(2)}) collective-permute-start(bf16[8,1632]{1,0:T(8,128)(2,1)S(1)} %get-tuple-element.16), channel_id=1, source_target_pairs={{9,0},{8,1},{11,2},{10,3},{13,4},{12,5},{15,6},{14,7},{17,8},{16,9... | collective-permute-start | bytes 78344 | tf_op jit(solution)/shard_map/ppermute | solution.py:300
  22.6 1.5 %collective-permute-done.6.refs_0_ = bf16[8,1632]{1,0:T(8,128)(2,1)S(1)} collective-permute-done((bf16[8,1632]{1,0:T(8,128)(2,1)S(1)}, bf16[8,1632]{1,0:T(8,128)(2,1)S(1)}, u32[]{:S(2)}, u32[]{:S(2)}) %collective-permute-start.6) | collective-permute-done | bytes 26144 | tf_op jit(solution)/shard_map/ppermute | solution.py:300
  24.1 0.0 collective-permute-done.7.refs_1_
  24.1 0.7 %shard_map.22 = f32[8,2,1632]{2,1,0:T(2,128)} custom-call(bf16[8,1632]{1,0:T(8,128)(2,1)S(1)} %collective-permute-done.6.refs_0_, bf16[8,1632]{1,0:T(8,128)(2,1)S(1)} %collective-permute-done.7.refs_1_), custom_call_target="tpu_custom_call" | custom-call | bytes 52224 | tf_op jit(solution)/shard_map/pallas_call | solution.py:265
  (2 shorter events, 0.1 us)
Async XLA Ops:
  0.0 2.2 %collective-permute-start = (f32[256,512]{1,0:T(8,128)}, f32[256,512]{1,0:T(8,128)S(1)}, u32[]{:S(2)}, u32[]{:S(2)}) collective-permute-start(f32[256,512]{1,0:T(8,128)} %x_ref.1), channel_id=1, source_target_pairs={{0,1},{1,0},{2,3},{3,2},{4,5},{5,4},{6,7},{7,6},{8,9},{9,8},{10,11... | collective-permute-start | bytes 1572872 | tf_op jit(solution)/shard_map/ppermute | solution.py:284
  0.5 1.0 %copy-start = (f32[256,512]{1,0:T(8,128)S(1)}, f32[256,512]{1,0:T(8,128)}, u32[]{:S(2)}) copy-start(f32[256,512]{1,0:T(8,128)} %x_ref.1) | copy-start | bytes 1572868
  2.4 6.9 %collective-permute-start.2 = (bf16[8,1280]{1,0:T(8,128)(2,1)S(1)}, bf16[8,1280]{1,0:T(8,128)(2,1)S(1)}, u32[]{:S(2)}, u32[]{:S(2)}) collective-permute-start(bf16[8,1280]{1,0:T(8,128)(2,1)S(1)} %shard_map.19), channel_id=1, source_target_pairs={{24,0},{0,8},{8,16},{16,24},{25,1},{1,9},{9,17},{17,25},{26,2},{2,... | collective-permute-start | bytes 61448 | tf_op jit(solution)/shard_map/ppermute | solution.py:290
  5.4 4.0 %collective-permute-start.1 = (bf16[8,1280]{1,0:T(8,128)(2,1)S(1)}, bf16[8,1280]{1,0:T(8,128)(2,1)S(1)}, u32[]{:S(2)}, u32[]{:S(2)}) collective-permute-start(bf16[8,1280]{1,0:T(8,128)(2,1)S(1)} %shard_map.19), channel_id=1, source_target_pairs={{8,0},{16,8},{24,16},{0,24},{9,1},{17,9},{25,17},{1,25},{10,2},{18... | collective-permute-start | bytes 61448 | tf_op jit(solution)/shard_map/ppermute | solution.py:290
  9.5 6.7 %collective-permute-start.3 = (bf16[48,1280]{1,0:T(8,128)(2,1)S(1)}, bf16[48,1280]{1,0:T(8,128)(2,1)S(1)}, u32[]{:S(2)}, u32[]{:S(2)}) collective-permute-start(bf16[48,1280]{1,0:T(8,128)(2,1)S(1)} %get-tuple-element.12), channel_id=1, source_target_pairs={{0,6},{1,7},{2,4},{3,5},{4,2},{5,3},{6,0},{7,1},{8,14},{9,15},{10,... | collective-permute-start | bytes 368648 | tf_op jit(solution)/shard_map/ppermute | solution.py:284
  12.0 5.4 %collective-permute-start.4 = (bf16[48,1280]{1,0:T(8,128)(2,1)S(1)}, bf16[48,1280]{1,0:T(8,128)(2,1)S(1)}, u32[]{:S(2)}, u32[]{:S(2)}) collective-permute-start(bf16[48,1280]{1,0:T(8,128)(2,1)S(1)} %get-tuple-element.13), channel_id=1, source_target_pairs={{0,2},{1,3},{2,0},{3,1},{4,6},{5,7},{6,4},{7,5},{8,10},{9,11},{10,... | collective-permute-start | bytes 368648 | tf_op jit(solution)/shard_map/ppermute | solution.py:284
  12.5 5.0 %collective-permute-start.5 = (bf16[48,1280]{1,0:T(8,128)(2,1)S(1)}, bf16[48,1280]{1,0:T(8,128)(2,1)S(1)}, u32[]{:S(2)}, u32[]{:S(2)}) collective-permute-start(bf16[48,1280]{1,0:T(8,128)(2,1)S(1)} %get-tuple-element.14), channel_id=1, source_target_pairs={{0,4},{1,5},{2,6},{3,7},{4,0},{5,1},{6,2},{7,3},{8,12},{9,13},{10,... | collective-permute-start | bytes 368648 | tf_op jit(solution)/shard_map/ppermute | solution.py:284
  19.0 5.1 %collective-permute-start.6 = (bf16[8,1632]{1,0:T(8,128)(2,1)S(1)}, bf16[8,1632]{1,0:T(8,128)(2,1)S(1)}, u32[]{:S(2)}, u32[]{:S(2)}) collective-permute-start(bf16[8,1632]{1,0:T(8,128)(2,1)S(1)} %get-tuple-element.15), channel_id=1, source_target_pairs={{25,0},{24,1},{27,2},{26,3},{29,4},{28,5},{31,6},{30,7},{1,8},{0,9... | collective-permute-start | bytes 78344 | tf_op jit(solution)/shard_map/ppermute | solution.py:300
  19.0 5.1 %collective-permute-start.7 = (bf16[8,1632]{1,0:T(8,128)(2,1)S(1)}, bf16[8,1632]{1,0:T(8,128)(2,1)S(1)}, u32[]{:S(2)}, u32[]{:S(2)}) collective-permute-start(bf16[8,1632]{1,0:T(8,128)(2,1)S(1)} %get-tuple-element.16), channel_id=1, source_target_pairs={{9,0},{8,1},{11,2},{10,3},{13,4},{12,5},{15,6},{14,7},{17,8},{16,9... | collective-permute-start | bytes 78344 | tf_op jit(solution)/shard_map/ppermute | solution.py:300

commit v6 on v2

--- a/solution.py
+++ b/solution.py
@@ -14,6 +14,7 @@
 LAGS = 51
 FINE = 8
 COARSE = -(-LAGS // FINE)
+MIDDLE = MAXLAG // FINE * FINE
 LANES = 128
 CORES = 2
 
@@ -176,17 +177,18 @@
     nothing = jnp.zeros((height, LANES), rows.dtype)
     if not shift:
         return jnp.concatenate([rows, nothing], axis=1)
+    amount = shift % LANES
     turned = [
-        pltpu.roll(rows[:, first : first + LANES], shift, 1)
+        pltpu.roll(rows[:, first : first + LANES], amount, 1)
         for first in range(0, length, LANES)
     ]
-    behind = lane_numbers(height, rows.dtype) >= shift
+    if shift > 0:
+        low, high = [nothing] + turned, turned + [nothing]
+    else:
+        low, high = turned + [nothing], turned[1:] + [nothing, turned[0]]
+    behind = lane_numbers(height, rows.dtype) >= amount
     return jnp.concatenate(
-        [
-            jnp.where(behind, here, before)
-            for before, here in zip([nothing] + turned, turned + [nothing])
-        ],
-        axis=1,
+        [jnp.where(behind, h, l) for l, h in zip(low, high)], axis=1
     )
 
 
@@ -200,8 +202,8 @@
     product = None
     for wide in finished_shards(runs, held):
         receivers, senders = wide[:group], wide[group:]
-        fine = [shifted(receivers, MAXLAG - j) for j in range(FINE)]
-        coarse = [shifted(senders, FINE * i) for i in range(COARSE)]
+        fine = [shifted(receivers, MAXLAG - MIDDLE - j) for j in range(FINE)]
+        coarse = [shifted(senders, FINE * i - MIDDLE) for i in range(COARSE)]
         term = lax.dot_general(
             jnp.concatenate(fine, axis=0).astype(jnp.bfloat16),
             jnp.concatenate(coarse, axis=0).astype(jnp.bfloat16),

time: 24.9 us -> 24.9 us (level)
  no operation moved by 1% of the time
where the time goes in v6:
time: 24.9 us; the launch traced here: 24.7 us
  starting transfers between devices  12.7 us (51%)
  waiting for transfers between devices  8.15 us (33%)
  Pallas kernels  2.82 us (11%)
  local copies, waits for them, and re-layouts  1.04 us (4%)
    ppermute x4, waiting for transfers between devices, swapped(): return lax.ppermute(block, axis, [(k, k ^ m) for k in devices])  5.18 us
    ppermute x2, starting transfers between devices, passed_along(): return lax.ppermute(block, 'chan', route)  5.09 us
    ppermute x4, starting transfers between devices, swapped(): return lax.ppermute(block, axis, [(k, k ^ m) for k in devices])  4.01 us
    ppermute x2, starting transfers between devices, passed_across(): return lax.ppermute(block, ('chan', 'tm'), route)  3.59 us
    pallas_call x6, Pallas kernels, call(): pl.pallas_call(kernel, out_shape=out_shape, in_specs=[spec] * len(inputs)...  2.82 us
    ppermute x2, waiting for transfers between devices, passed_across(): return lax.ppermute(block, ('chan', 'tm'), route)  1.54 us
    ppermute x2, waiting for transfers between devices, passed_along(): return lax.ppermute(block, 'chan', route)  1.43 us
    unnamed x2, local copies, waits for them, and re-layouts  1.04 us
  transfers between devices with their start and end apart: 8, of which 7 were waited for; matrix products, arithmetic and copies ran while one was open for 0% of the time, Pallas kernels for 2%

profile of v6, /device:TPU:0, one launch (start us, length us, event | category | flops | bytes accessed | tf_op | source)
XLA Modules:
  0.0 24.7 jit_solution(11873254591601220800)
XLA Ops:
  0.0 0.5 %collective-permute-start = (f32[256,512]{1,0:T(8,128)}, f32[256,512]{1,0:T(8,128)S(1)}, u32[]{:S(2)}, u32[]{:S(2)}) collective-permute-start(f32[256,512]{1,0:T(8,128)} %x_ref.1), channel_id=1, source_target_pairs={{0,1},{1,0},{2,3},{3,2},{4,5},{5,4},{6,7},{7,6},{8,9},{9,8},{10,11... | collective-permute-start | bytes 1572872 | tf_op jit(solution)/shard_map/ppermute | solution.py:282
  0.5 0.0 copy-start
  0.5 1.0 %copy-done = f32[256,512]{1,0:T(8,128)S(1)} copy-done((f32[256,512]{1,0:T(8,128)S(1)}, f32[256,512]{1,0:T(8,128)}, u32[]{:S(2)}) %copy-start) | copy-done | bytes 524312
  1.5 0.7 %collective-permute-done.other_ref = f32[256,512]{1,0:T(8,128)S(1)} collective-permute-done((f32[256,512]{1,0:T(8,128)}, f32[256,512]{1,0:T(8,128)S(1)}, u32[]{:S(2)}, u32[]{:S(2)}) %collective-permute-start) | collective-permute-done | bytes 524320 | tf_op jit(solution)/shard_map/ppermute | solution.py:282
  2.2 0.2 shard_map.19
  2.4 3.0 %collective-permute-start.2 = (bf16[8,1280]{1,0:T(8,128)(2,1)S(1)}, bf16[8,1280]{1,0:T(8,128)(2,1)S(1)}, u32[]{:S(2)}, u32[]{:S(2)}) collective-permute-start(bf16[8,1280]{1,0:T(8,128)(2,1)S(1)} %shard_map.19), channel_id=1, source_target_pairs={{24,0},{0,8},{8,16},{16,24},{25,1},{1,9},{9,17},{17,25},{26,2},{2,... | collective-permute-start | bytes 61448 | tf_op jit(solution)/shard_map/ppermute | solution.py:288
  5.4 2.1 %collective-permute-start.1 = (bf16[8,1280]{1,0:T(8,128)(2,1)S(1)}, bf16[8,1280]{1,0:T(8,128)(2,1)S(1)}, u32[]{:S(2)}, u32[]{:S(2)}) collective-permute-start(bf16[8,1280]{1,0:T(8,128)(2,1)S(1)} %shard_map.19), channel_id=1, source_target_pairs={{8,0},{16,8},{24,16},{0,24},{9,1},{17,9},{25,17},{1,25},{10,2},{18... | collective-permute-start | bytes 61448 | tf_op jit(solution)/shard_map/ppermute | solution.py:288
  7.5 0.5 %shard_map.18.receivers_ref = bf16[128,1280]{1,0:T(8,128)(2,1)S(1)} custom-call(f32[136,512]{1,0:T(8,128)S(1)} %shard_map.17.own_ref, f32[256,512]{1,0:T(8,128)S(1)} %collective-permute-done.other_ref), custom_call_target="tpu_custom_call" | custom-call | flops 536870912 | bytes 802816 | tf_op jit(solution)/shard_map/pallas_call | solution.py:267
  8.0 1.3 %collective-permute-done.2.refs_1_ = bf16[8,1280]{1,0:T(8,128)(2,1)S(1)} collective-permute-done((bf16[8,1280]{1,0:T(8,128)(2,1)S(1)}, bf16[8,1280]{1,0:T(8,128)(2,1)S(1)}, u32[]{:S(2)}, u32[]{:S(2)}) %collective-permute-start.2) | collective-permute-done | bytes 20512 | tf_op jit(solution)/shard_map/ppermute | solution.py:288
  9.3 0.1 collective-permute-done.1.refs_0_
  9.5 2.5 %collective-permute-start.3 = (bf16[48,1280]{1,0:T(8,128)(2,1)S(1)}, bf16[48,1280]{1,0:T(8,128)(2,1)S(1)}, u32[]{:S(2)}, u32[]{:S(2)}) collective-permute-start(bf16[48,1280]{1,0:T(8,128)(2,1)S(1)} %get-tuple-element.12), channel_id=1, source_target_pairs={{0,6},{1,7},{2,4},{3,5},{4,2},{5,3},{6,0},{7,1},{8,14},{9,15},{10,... | collective-permute-start | bytes 368648 | tf_op jit(solution)/shard_map/ppermute | solution.py:282
  12.0 0.5 %collective-permute-start.4 = (bf16[48,1280]{1,0:T(8,128)(2,1)S(1)}, bf16[48,1280]{1,0:T(8,128)(2,1)S(1)}, u32[]{:S(2)}, u32[]{:S(2)}) collective-permute-start(bf16[48,1280]{1,0:T(8,128)(2,1)S(1)} %get-tuple-element.13), channel_id=1, source_target_pairs={{0,4},{1,5},{2,6},{3,7},{4,0},{5,1},{6,2},{7,3},{8,12},{9,13},{10,... | collective-permute-start | bytes 368648 | tf_op jit(solution)/shard_map/ppermute | solution.py:282
  12.5 0.5 %collective-permute-start.5 = (bf16[48,1280]{1,0:T(8,128)(2,1)S(1)}, bf16[48,1280]{1,0:T(8,128)(2,1)S(1)}, u32[]{:S(2)}, u32[]{:S(2)}) collective-permute-start(bf16[48,1280]{1,0:T(8,128)(2,1)S(1)} %get-tuple-element.14), channel_id=1, source_target_pairs={{0,2},{1,3},{2,0},{3,1},{4,6},{5,7},{6,4},{7,5},{8,10},{9,11},{10,... | collective-permute-start | bytes 368648 | tf_op jit(solution)/shard_map/ppermute | solution.py:282
  13.0 3.1 %collective-permute-done.3.refs_1_ = bf16[48,1280]{1,0:T(8,128)(2,1)S(1)} collective-permute-done((bf16[48,1280]{1,0:T(8,128)(2,1)S(1)}, bf16[48,1280]{1,0:T(8,128)(2,1)S(1)}, u32[]{:S(2)}, u32[]{:S(2)}) %collective-permute-start.3) | collective-permute-done | bytes 122912 | tf_op jit(solution)/shard_map/ppermute | solution.py:282
  16.1 1.2 %collective-permute-done.4.refs_2_ = bf16[48,1280]{1,0:T(8,128)(2,1)S(1)} collective-permute-done((bf16[48,1280]{1,0:T(8,128)(2,1)S(1)}, bf16[48,1280]{1,0:T(8,128)(2,1)S(1)}, u32[]{:S(2)}, u32[]{:S(2)}) %collective-permute-start.4) | collective-permute-done | bytes 122912 | tf_op jit(solution)/shard_map/ppermute | solution.py:282
  17.3 0.2 collective-permute-done.5.refs_3_
  17.5 1.4 %shard_map.21 = (bf16[8,1632]{1,0:T(8,128)(2,1)S(1)}, bf16[8,1632]{1,0:T(8,128)(2,1)S(1)}) custom-call(bf16[48,1280]{1,0:T(8,128)(2,1)S(1)} %get-tuple-element.11.refs_0_, bf16[48,1280]{1,0:T(8,128)(2,1)S(1)} %collective-permute-done.3.refs_1_, bf16[48,1280]{1,0:T(8,128)(2,1)S(1)} %collective-permute-done.4.refs_2_, ...), custom_call_target="tpu_custom_call" | custom-call | flops 293601280 | bytes 491520 | tf_op jit(solution)/shard_map/pallas_call | solution.py:267
  18.9 0.1 collective-permute-start.6
  19.0 3.5 %collective-permute-start.7 = (bf16[8,1632]{1,0:T(8,128)(2,1)S(1)}, bf16[8,1632]{1,0:T(8,128)(2,1)S(1)}, u32[]{:S(2)}, u32[]{:S(2)}) collective-permute-start(bf16[8,1632]{1,0:T(8,128)(2,1)S(1)} %get-tuple-element.16), channel_id=1, source_target_pairs={{9,0},{8,1},{11,2},{10,3},{13,4},{12,5},{15,6},{14,7},{17,8},{16,9... | collective-permute-start | bytes 78344 | tf_op jit(solution)/shard_map/ppermute | solution.py:298
  22.5 1.5 %collective-permute-done.6.refs_0_ = bf16[8,1632]{1,0:T(8,128)(2,1)S(1)} collective-permute-done((bf16[8,1632]{1,0:T(8,128)(2,1)S(1)}, bf16[8,1632]{1,0:T(8,128)(2,1)S(1)}, u32[]{:S(2)}, u32[]{:S(2)}) %collective-permute-start.6) | collective-permute-done | bytes 26144 | tf_op jit(solution)/shard_map/ppermute | solution.py:298
  24.1 0.0 collective-permute-done.7.refs_1_
  24.1 0.7 %shard_map.22 = f32[8,2,1632]{2,1,0:T(2,128)} custom-call(bf16[8,1632]{1,0:T(8,128)(2,1)S(1)} %collective-permute-done.6.refs_0_, bf16[8,1632]{1,0:T(8,128)(2,1)S(1)} %collective-permute-done.7.refs_1_), custom_call_target="tpu_custom_call" | custom-call | bytes 52224 | tf_op jit(solution)/shard_map/pallas_call | solution.py:267
  (2 shorter events, 0.1 us)
Async XLA Ops:
  0.0 2.2 %collective-permute-start = (f32[256,512]{1,0:T(8,128)}, f32[256,512]{1,0:T(8,128)S(1)}, u32[]{:S(2)}, u32[]{:S(2)}) collective-permute-start(f32[256,512]{1,0:T(8,128)} %x_ref.1), channel_id=1, source_target_pairs={{0,1},{1,0},{2,3},{3,2},{4,5},{5,4},{6,7},{7,6},{8,9},{9,8},{10,11... | collective-permute-start | bytes 1572872 | tf_op jit(solution)/shard_map/ppermute | solution.py:282
  0.5 1.0 %copy-start = (f32[256,512]{1,0:T(8,128)S(1)}, f32[256,512]{1,0:T(8,128)}, u32[]{:S(2)}) copy-start(f32[256,512]{1,0:T(8,128)} %x_ref.1) | copy-start | bytes 1572868
  2.4 6.9 %collective-permute-start.2 = (bf16[8,1280]{1,0:T(8,128)(2,1)S(1)}, bf16[8,1280]{1,0:T(8,128)(2,1)S(1)}, u32[]{:S(2)}, u32[]{:S(2)}) collective-permute-start(bf16[8,1280]{1,0:T(8,128)(2,1)S(1)} %shard_map.19), channel_id=1, source_target_pairs={{24,0},{0,8},{8,16},{16,24},{25,1},{1,9},{9,17},{17,25},{26,2},{2,... | collective-permute-start | bytes 61448 | tf_op jit(solution)/shard_map/ppermute | solution.py:288
  5.4 4.0 %collective-permute-start.1 = (bf16[8,1280]{1,0:T(8,128)(2,1)S(1)}, bf16[8,1280]{1,0:T(8,128)(2,1)S(1)}, u32[]{:S(2)}, u32[]{:S(2)}) collective-permute-start(bf16[8,1280]{1,0:T(8,128)(2,1)S(1)} %shard_map.19), channel_id=1, source_target_pairs={{8,0},{16,8},{24,16},{0,24},{9,1},{17,9},{25,17},{1,25},{10,2},{18... | collective-permute-start | bytes 61448 | tf_op jit(solution)/shard_map/ppermute | solution.py:288
  9.5 6.7 %collective-permute-start.3 = (bf16[48,1280]{1,0:T(8,128)(2,1)S(1)}, bf16[48,1280]{1,0:T(8,128)(2,1)S(1)}, u32[]{:S(2)}, u32[]{:S(2)}) collective-permute-start(bf16[48,1280]{1,0:T(8,128)(2,1)S(1)} %get-tuple-element.12), channel_id=1, source_target_pairs={{0,6},{1,7},{2,4},{3,5},{4,2},{5,3},{6,0},{7,1},{8,14},{9,15},{10,... | collective-permute-start | bytes 368648 | tf_op jit(solution)/shard_map/ppermute | solution.py:282
  12.0 5.4 %collective-permute-start.4 = (bf16[48,1280]{1,0:T(8,128)(2,1)S(1)}, bf16[48,1280]{1,0:T(8,128)(2,1)S(1)}, u32[]{:S(2)}, u32[]{:S(2)}) collective-permute-start(bf16[48,1280]{1,0:T(8,128)(2,1)S(1)} %get-tuple-element.13), channel_id=1, source_target_pairs={{0,4},{1,5},{2,6},{3,7},{4,0},{5,1},{6,2},{7,3},{8,12},{9,13},{10,... | collective-permute-start | bytes 368648 | tf_op jit(solution)/shard_map/ppermute | solution.py:282
  12.5 5.0 %collective-permute-start.5 = (bf16[48,1280]{1,0:T(8,128)(2,1)S(1)}, bf16[48,1280]{1,0:T(8,128)(2,1)S(1)}, u32[]{:S(2)}, u32[]{:S(2)}) collective-permute-start(bf16[48,1280]{1,0:T(8,128)(2,1)S(1)} %get-tuple-element.14), channel_id=1, source_target_pairs={{0,2},{1,3},{2,0},{3,1},{4,6},{5,7},{6,4},{7,5},{8,10},{9,11},{10,... | collective-permute-start | bytes 368648 | tf_op jit(solution)/shard_map/ppermute | solution.py:282
  18.9 5.1 %collective-permute-start.6 = (bf16[8,1632]{1,0:T(8,128)(2,1)S(1)}, bf16[8,1632]{1,0:T(8,128)(2,1)S(1)}, u32[]{:S(2)}, u32[]{:S(2)}) collective-permute-start(bf16[8,1632]{1,0:T(8,128)(2,1)S(1)} %get-tuple-element.15), channel_id=1, source_target_pairs={{25,0},{24,1},{27,2},{26,3},{29,4},{28,5},{31,6},{30,7},{1,8},{0,9... | collective-permute-start | bytes 78344 | tf_op jit(solution)/shard_map/ppermute | solution.py:298
  19.0 5.1 %collective-permute-start.7 = (bf16[8,1632]{1,0:T(8,128)(2,1)S(1)}, bf16[8,1632]{1,0:T(8,128)(2,1)S(1)}, u32[]{:S(2)}, u32[]{:S(2)}) collective-permute-start(bf16[8,1632]{1,0:T(8,128)(2,1)S(1)} %get-tuple-element.16), channel_id=1, source_target_pairs={{9,0},{8,1},{11,2},{10,3},{13,4},{12,5},{15,6},{14,7},{17,8},{16,9... | collective-permute-start | bytes 78344 | tf_op jit(solution)/shard_map/ppermute | solution.py:298
